TPU v7x, 32 devices: a whole 2x2x4 slice. The times are simulated.
32 devices in a mesh: nodes: 8 (over z, x), cams: 4 (over y, core).
Axes of the slice: x: 2, y: 2, z: 4, core: 2. Of those that a mesh axis runs over, the one named last changes fastest.
Arguments:
- iterate: float32 [64, 12, 128], P(('nodes', 'cams')), may hold values from -6 to 6
- residual: float32 [64, 12, 128], P(('nodes', 'cams')), may hold values from -6 to 6
- direction: float32 [64, 12, 128], P(('nodes', 'cams')), may hold values from -5 to 5
- precond: float32 [64, 12, 128], P(('nodes', 'cams')), may hold values from 0.2 to 6, as said below
- send_list: int32 [8, 8, 3], P('nodes'), may hold values from -1 to 7, as said below
- grads: bfloat16 [12, 65536], P(None, ('nodes', 'cams')), may hold values from -2.390625 to 2.390625
- node_refs: int32 [4, 65536], P(None, ('nodes', 'cams')), may hold values from 0 to 3071, as said below
- skin: bfloat16 [4, 65536], P(None, ('nodes', 'cams')), may hold values from 0.099609375 to 1
- rigid_nbr: int32 [64, 6, 128], P(('nodes', 'cams')), may hold values from 0 to 127, as said below
Outputs:
- new_iterate: float32 [64, 12, 128], P(('nodes', 'cams'))
- new_residual: float32 [64, 12, 128], P(('nodes', 'cams'))
- new_direction: float32 [64, 12, 128], P(('nodes', 'cams'))
Inputs may be any that keep to these rules, and one draw needn't show every extreme that they name: `precond`: Positive. `send_list`: for each owner and receiver the live entries come first and the rest are -1; at most 3 live entries, and every receiver n has all 3 slots live from owner (n - 1) mod 8. `node_refs`: every reference names a live slot of its device's receiver; the 4 references of a pixel lie in the same slot. `rigid_nbr`: never the node itself.
All inputs are finite; a program needn't handle non-finite values.
Results may differ from a plain program's by a relative error of at most 0.00085.
Values sent between devices are 32-bit elements; how exact they have to be, the bound alone decides.
No kernel may reach another device: no remote copies, remote signals or barrier semaphores. Data moves between devices by JAX's collectives and lax.ppermute only.
A program may use at most 64 MiB of HBM per device.

v0:
```python
import functools

import jax
import jax.numpy as jnp
from jax import lax
from jax.experimental import pallas as pl
from jax.experimental.pallas import tpu as pltpu
from jax.sharding import PartitionSpec as P

FRAMES = 8
AXES = ("nodes", "cams")
temporal_weight = 0.5
rigid_weight = 0.1
NN = (((1,), (0,)), ((), ()))
NT = (((1,), (1,)), ((), ()))
LANES = 128
HALF = 8
f32 = jnp.float32
bf16 = jnp.bfloat16

VMEM = pl.BlockSpec(memory_space=pltpu.VMEM)
SMEM = pl.BlockSpec(memory_space=pltpu.SMEM)


def limit(slots, pixels):
    need = 8 * 2**20 + slots * 2 * HALF * pixels * 3
    return pltpu.CompilerParams(vmem_limit_bytes=min(need, 56 * 2**20))


def halves(value):
    high = value.astype(bf16)
    low = (value - high.astype(f32)).astype(bf16)
    return high, low


def rows_sum(value):
    return jnp.sum(value, axis=0, keepdims=True)


def loop(count, body):
    lax.fori_loop(0, count, lambda i, carry: (body(i), carry)[1], 0, unroll=count <= 32)


def pack_kernel(sizes, owners, cams, extra, source, out, halves_of, lists):
    rows, slot_count, piece, pieces, half_pieces = sizes
    half_rows = half_pieces * piece
    lists[...] = jnp.zeros_like(lists)
    for s in range(slot_count):
        row, lane = divmod(s * owners, LANES)
        moved = source[rows + s : rows + s + 1, :]
        if lane:
            moved = pltpu.roll(moved, lane, 1)
        lists[row : row + 1, :] = lists[row : row + 1, :] + moved
    size = half_rows + extra
    halves_of[...] = jnp.zeros_like(halves_of)
    for c in range(pieces):
        at = (c % 2) * size + (c // 2) * piece
        halves_of[at : at + piece, :] = source[c * piece : (c + 1) * piece, :]
    for parity in range(2):
        at = parity * size + half_rows
        halves_of[at : at + extra, :] = lists[0:extra, :]

    def write(owner):
        for c in range(cams):
            at = (c % 2) * size
            out[pl.ds((owner * cams + c) * size, size), :] = halves_of[at : at + size, :]

    loop(owners, write)


def near_kernel(sizes, rows, edges, send_list, joined, sums_out, choose, *pieces):
    owners, cams, slot_count, held, params, part, half_pieces, extra, back_rows, step = sizes
    piece = held * part
    *pieces, near_rows = pieces
    value = joined[0:rows, :]
    left = joined[rows : 2 * rows, :]
    scale = joined[2 * rows : 3 * rows, :]
    high, low = halves(value)
    stack = jnp.concatenate([high.astype(f32), low.astype(f32), jnp.ones((16, LANES), f32)], axis=0)
    stack = stack.astype(bf16)
    node_rows = lax.broadcasted_iota(jnp.int32, (LANES, LANES), 0).astype(f32)
    patch_row = lax.broadcasted_iota(jnp.int32, (rows, LANES), 0) % held
    rigid = jnp.zeros_like(value)
    for q in range(held):
        hits = jnp.zeros((LANES, LANES), f32)
        for r in range(edges):
            at = 3 * rows + r * held + q
            hits = hits + jnp.where(node_rows == joined[at : at + 1, :], 1.0, 0.0)
        hits = hits.astype(bf16)
        pulled = lax.dot_general(stack, hits, NN, preferred_element_type=f32)
        pushed = lax.dot_general(stack, hits, NT, preferred_element_type=f32)
        degree = pushed[2 * rows : 2 * rows + 1]
        both = pulled + pushed
        edge_sum = value * (degree + float(edges)) - (both[:rows] + both[rows : 2 * rows])
        rigid = jnp.where(patch_row == q, edge_sum, rigid)
    near = rigid_weight * rigid + (2.0 * temporal_weight) * value
    near_rows[...] = near
    cam = lax.axis_index("cams")
    for distance, out in enumerate(pieces):
        target = lax.rem(cam + distance, cams) * piece
        offset = jnp.minimum(target, rows - piece)
        out[0:piece, :] = joined[pl.ds(rows + offset, piece), :]
        out[piece : 2 * piece, :] = joined[pl.ds(2 * rows + offset, piece), :]
        out[2 * piece : 3 * piece, :] = near_rows[pl.ds(offset, piece), :]
        if cams * piece > rows:

            @pl.when(target >= rows)
            def _():
                out[...] = jnp.zeros_like(out)

    sums_out[0:1, :] = rows_sum(left * (scale * left))
    sums_out[1:2, :] = rows_sum(value * near)

    column = lax.broadcasted_iota(jnp.int32, (1, choose.shape[1]), 1)
    row = column % back_rows
    slot = column // (back_rows * cams) * slot_count + row // part
    slot = jnp.where(row < slot_count * part, slot, -1)
    listed = jnp.zeros_like(column)
    for owner in range(owners):
        for s in range(slot_count):
            patch = jnp.maximum(send_list[s, 0, owner], 0)
            listed = jnp.where(slot == owner * slot_count + s, patch, listed)
    target = listed // held * piece + row % part * held + listed % held
    target = jnp.where(slot >= 0, target, cams * piece)
    image_row = lax.broadcasted_iota(jnp.int32, choose.shape, 0)
    choose[...] = jnp.where(image_row == target, 1.0, 0.0).astype(bf16)


def masks_kernel(params, refs_count, part, half_pieces, pixel_rows, spread_out, masked, grads_pad):
    pixels = pixel_rows.shape[1]
    side = masked.shape[0] // 2
    chunk = 512
    grads_pad[...] = jnp.zeros_like(grads_pad)
    for c in range(params // part):
        for copy in range(2):
            at = (2 * (c % 2) + copy) * HALF + (c // 2) * part
            grads_pad[at : at + part, :] = pixel_rows[c * part : (c + 1) * part, :]
    node_rows = lax.broadcasted_iota(jnp.int32, (LANES, chunk), 0)
    upper = lax.broadcasted_iota(jnp.int32, (2 * HALF, chunk), 0) // HALF
    for at in range(0, pixels, chunk):
        cols = slice(at, at + chunk)
        weights = pixel_rows[params : params + refs_count, cols]
        refs = pixel_rows[params + refs_count : params + 2 * refs_count, cols].astype(jnp.int32)
        node = lax.bitwise_and(refs, LANES - 1)
        slot_of = lax.shift_right_logical(refs[0:1], 7) - upper
        even, odd = grads_pad[0 : 2 * HALF, cols], grads_pad[2 * HALF :, cols]
        spread = jnp.where(node_rows == node[0:1], weights[0:1], 0.0)
        for k in range(1, refs.shape[0]):
            spread = spread + jnp.where(node_rows == node[k : k + 1], weights[k : k + 1], 0.0)
        spread_out[:, cols] = spread

        def mask(pair):
            here = slot_of == 2 * pair
            rows = pl.multiple_of(2 * HALF * pair, 2 * HALF)
            masked[pl.ds(rows, 2 * HALF), cols] = jnp.where(here, even, 0.0).astype(bf16)
            rows = pl.multiple_of(side + 2 * HALF * pair, 2 * HALF)
            masked[pl.ds(rows, 2 * HALF), cols] = jnp.where(here, odd, 0.0).astype(bf16)

        loop(side // (2 * HALF), mask)


def table_kernel(sizes, gathered, table_out, frames_out, sums_out):
    owners, cams, slot_count, held, params, part, half_pieces, extra, back_rows, step = sizes
    devices = owners * cams
    piece = held * part
    half = half_pieces * part
    block_rows = half * held + extra
    receiver = lax.axis_index("nodes")
    cam = lax.axis_index("cams")
    curvature = jnp.zeros((1, LANES), f32)
    inside = cam * part < params
    offset = jnp.minimum(cam // 2, half_pieces - 1) * piece
    for c in range(cams):
        device = receiver * cams + c
        value = gathered[pl.ds(device * block_rows + offset, piece), :]
        before = gathered[pl.ds(jnp.maximum(device - step, 0) * block_rows + offset, piece), :]
        after = gathered[
            pl.ds(jnp.minimum(device + step, devices - 1) * block_rows + offset, piece), :
        ]
        earlier = jnp.where(jnp.logical_and(inside, device >= step), before, 0.0)
        following = jnp.where(jnp.logical_and(inside, device + step < devices), after, 0.0)
        frames = -temporal_weight * (earlier + following)
        frames_out[c * piece : (c + 1) * piece, :] = frames
        curvature = curvature + rows_sum(value * frames)
    sums_out[0:1, :] = curvature

    owner_rows = cams * block_rows
    table_row = lax.broadcasted_iota(jnp.int32, (slot_count * HALF, 1), 0)
    within = table_row % HALF
    lane_of = lax.broadcasted_iota(jnp.int32, (slot_count * HALF, LANES), 1)
    entry = table_row // HALF * owners + receiver
    column = lax.broadcasted_iota(jnp.int32, (slot_count * HALF, owner_rows), 1)
    list_row = [lane_of + line * LANES == entry for line in range(extra)]

    def fetch(owner):
        at = owner * owner_rows
        listed = jnp.zeros((slot_count * HALF, LANES), f32)
        for line in range(extra):
            row = gathered[pl.ds(at + half * held + line, 1), :]
            listed = listed + jnp.where(list_row[line], row, 0.0)
        listed = jnp.maximum(jnp.sum(listed, axis=1, keepdims=True), 0.0).astype(jnp.int32)
        source = listed // held * block_rows + listed % held + within * held
        source = jnp.where(within < half, source, -1)
        choose = jnp.where(column == source, 1.0, 0.0).astype(bf16)
        high, low = halves(gathered[pl.ds(at, owner_rows), :])
        picked = lax.dot_general(choose, high, NN, preferred_element_type=f32)
        picked = picked + lax.dot_general(choose, low, NN, preferred_element_type=f32)
        rows = pl.multiple_of(owner * slot_count * HALF, HALF)
        table_out[pl.ds(rows, slot_count * HALF), :] = picked

    filled = owners * slot_count * HALF
    if table_out.shape[0] > filled:
        table_out[filled:, :] = jnp.zeros((table_out.shape[0] - filled, LANES), f32)
    loop(owners, fetch)


def pull(table, masked, parity, cols):
    side = masked.shape[0] // 2
    live = masked[pl.ds(pl.multiple_of(parity * side, 2 * HALF), side), cols]
    pulled = lax.dot_general(table, live, NN, preferred_element_type=f32)
    return pulled[:LANES] + pulled[LANES:]


def turned_halves(table):
    return jnp.concatenate(halves(table[...].T), axis=0)


def own_kernel(table, masked, pulled_out):
    parity = lax.rem(lax.axis_index("cams"), 2)
    turned_table = turned_halves(table)
    chunk = 512
    for at in range(0, masked.shape[1], chunk):
        cols = slice(at, at + chunk)
        pulled_out[:, cols] = pull(turned_table, masked, parity, cols)


def data_kernel(sizes, pulled_own, table, near_sums, frame_sums, spread, masked, out, products):
    owners, cams, slot_count, held, params, part, half_pieces, extra, back_rows, step = sizes
    side = masked.shape[0] // 2
    parity = 1 - lax.rem(lax.axis_index("cams"), 2)
    turned_table = turned_halves(table)
    curvature = near_sums[1:2, :] + frame_sums[0:1, :]
    chunk = 512
    for at in range(0, spread.shape[1], chunk):
        cols = slice(at, at + chunk)
        weights = spread[:, cols]
        pulled = pulled_own[:, cols] + pull(turned_table, masked, parity, cols)
        projected = rows_sum(weights * pulled)
        squared = projected * projected
        for lane in range(0, chunk, LANES):
            curvature = curvature + squared[:, lane : lane + LANES]
        both = jnp.concatenate(halves(weights * projected), axis=0)
        back = lax.dot_general(masked[:, cols], both, NT, preferred_element_type=f32)
        back = back[:, :LANES] + back[:, LANES:]
        if at == 0:
            products[...] = back
        else:
            products[...] += back

    middle = LANES // 2
    lane_of = lax.broadcasted_iota(jnp.int32, (1, LANES), 1)
    start = near_sums[0:1, :]
    start = start + pltpu.roll(start, middle, 1)
    curvature = curvature + pltpu.roll(curvature, middle, 1)
    scalars = jnp.where(lane_of < middle, start, curvature)

    def give(owner):
        for c in range(cams):
            base = (owner * cams + c) * back_rows
            for s in range(slot_count):
                if c * part < params:
                    at = (c % 2) * side + (owner * slot_count + s) * HALF + (c // 2) * part
                    value = products[pl.ds(at, part), :]
                else:
                    value = jnp.zeros((part, LANES), f32)
                out[pl.ds(base + s * part, part), :] = value
            out[pl.ds(base + slot_count * part, 1), :] = scalars

    loop(owners, give)


def image_kernel(sizes, choose, received, frames, *refs):
    owners, cams, slot_count, held, params, part, half_pieces, extra, back_rows, step = sizes
    mine, (scalars, blocks, image) = refs[:cams], refs[cams:]
    cam = lax.axis_index("cams")
    piece = held * part
    value = received[...]
    high, rest = halves(value)
    low = (value - high.astype(f32) - rest.astype(f32)).astype(bf16)
    total = sum(
        lax.dot_general(choose[...], term, NN, preferred_element_type=f32)
        for term in (high, rest, low)
    )
    image[...] = total[0 : cams * piece]
    last = total[cams * piece : cams * piece + 1]
    half = LANES // 2
    lane_of = lax.broadcasted_iota(jnp.int32, (1, LANES), 1)
    start = jnp.sum(jnp.where(lane_of < half, last, 0.0), axis=1, keepdims=True)
    curvature = jnp.sum(jnp.where(lane_of < half, 0.0, last), axis=1, keepdims=True)
    length = start / curvature
    norms = jnp.zeros((1, LANES), f32)
    for distance, block in enumerate(mine):
        rows = pl.ds(lax.rem(cam + cams - distance, cams) * piece, piece)
        residual, precond, near = (block[k * piece : (k + 1) * piece, :] for k in range(3))
        value = image[rows, :] + near + frames[rows, :]
        image[rows, :] = value
        left = residual - length * value
        norms = norms + rows_sum(left * (precond * left))
    scalars[0:1, :] = jnp.broadcast_to(start, (1, LANES))
    scalars[1:2, :] = jnp.broadcast_to(length, (1, LANES))

    def tell(owner):
        for c in range(cams):
            base = (owner * cams + c) * (piece + 1)
            blocks[pl.ds(base, 1), :] = norms
            blocks[pl.ds(base + 1, piece), :] = image[c * piece : (c + 1) * piece, :]

    loop(owners, tell)


def update_kernel(
    sizes, arrived, scalars, iterate, residual, direction, precond,
    new_iterate, new_residual, new_direction,
):
    owners, cams, slot_count, held, params, part, half_pieces, extra, back_rows, step = sizes
    piece = held * part
    rows = iterate.shape[0]
    own = lax.axis_index("nodes")
    norms = arrived[0:1, :]
    for device in range(1, owners * cams):
        norms = norms + arrived[device * (piece + 1) : device * (piece + 1) + 1, :]
    start, length = scalars[0:1, :], scalars[1:2, :]
    ratio = jnp.sum(norms, axis=1, keepdims=True) / start
    for c in range(rows // piece):
        here = slice(c * piece, (c + 1) * piece)
        image = arrived[pl.ds((own * cams + c) * (piece + 1) + 1, piece), :]
        value = direction[here, :]
        left = residual[here, :] - length * image
        new_iterate[here, :] = iterate[here, :] + length * value
        new_residual[here, :] = left
        new_direction[here, :] = precond[here, :] * left + ratio * value


def flat(value):
    return jnp.transpose(value, (1, 0, 2)).reshape(-1, value.shape[2])


def joined_rows(parts):
    count = -(-sum(part.shape[0] for part in parts) // 8) * 8
    width = max(part.shape[-1] for part in parts)
    total, at = None, 0
    for part in parts:
        sides = [(at, count - at - part.shape[0], 0)] + [(0, 0, 0)] * (part.ndim - 1)
        sides[-1] = (0, width - part.shape[-1], 0)
        value = lax.pad(part, jnp.zeros((), part.dtype), sides).astype(f32)
        total = value if total is None else total + value
        at += part.shape[0]
    return total


def exchange(blocks, axes):
    rows, lanes = blocks.shape
    peers = lax.axis_size(axes)
    blocks = blocks.reshape(peers, rows // peers, 1, lanes)
    blocks = lax.all_to_all(blocks, axes, split_axis=0, concat_axis=0, tiled=True)
    return blocks.reshape(rows, lanes)


def on_device(iterate, residual, direction, precond, send_list, grads, node_refs, skin, rigid_nbr):
    held, params, lanes = direction.shape
    pixels = grads.shape[1]
    owners = lax.axis_size("nodes")
    cams = lax.axis_size("cams")
    devices = owners * cams
    slot_count = send_list.shape[2]
    slots = owners * slot_count
    asked = limit(slots, pixels)
    rows = held * params
    extra = -(-slots // lanes)
    part = next(n for n in range(1, params + 1) if params % n == 0 and n * cams >= params)
    piece = held * part
    back_rows = slot_count * part + 1
    half_pieces = -(-(params // part) // 2)
    side = (slots + slots % 2) * HALF
    sizes = (
        owners, cams, slot_count, held, params, part, half_pieces, extra, back_rows, devices // FRAMES
    )

    def array(count):
        return jax.ShapeDtypeStruct((count, lanes), f32)

    iterate, residual, direction, precond = (flat(v) for v in (iterate, residual, direction, precond))
    by_slot = jnp.transpose(send_list, (2, 0, 1))
    source = joined_rows((direction.reshape(rows, 1, lanes), by_slot))
    size = half_pieces * piece + extra
    packed = pl.pallas_call(
        functools.partial(
            pack_kernel, (rows, slot_count, piece, params // part, half_pieces), owners, cams, extra
        ),
        out_shape=array(devices * size),
        in_specs=[VMEM],
        out_specs=VMEM,
        scratch_shapes=[
            pltpu.VMEM((-(-2 * size // 8) * 8, lanes), f32),
            pltpu.VMEM((-(-extra // 8) * 8, lanes), f32),
        ],
        compiler_params=asked,
        name="pack",
    )(source.reshape(-1, lanes))
    packed, rigid_nbr, node_refs = lax.optimization_barrier((packed, rigid_nbr, node_refs))
    gathered = exchange(packed, AXES)

    joined = joined_rows(
        [v.reshape(params, held, lanes) for v in (direction, residual, precond)]
        + [jnp.transpose(rigid_nbr, (1, 0, 2))]
    ).reshape(-1, lanes)
    image_rows = -(-(cams * piece + 1) // 16) * 16
    sums, choose, *pieces = pl.pallas_call(
        functools.partial(near_kernel, sizes, rows, rigid_nbr.shape[1]),
        out_shape=(array(8), jax.ShapeDtypeStruct((image_rows, devices * back_rows), bf16))
        + (array(3 * piece),) * cams,
        in_specs=[SMEM, VMEM],
        out_specs=(VMEM,) * (2 + cams),
        scratch_shapes=[pltpu.VMEM((rows, lanes), f32)],
        compiler_params=asked,
        name="near",
    )(by_slot, joined)
    spread, masked = pl.pallas_call(
        functools.partial(masks_kernel, params, node_refs.shape[0], part, half_pieces),
        out_shape=(
            jax.ShapeDtypeStruct((lanes, pixels), f32),
            jax.ShapeDtypeStruct((2 * side, pixels), bf16),
        ),
        in_specs=[VMEM],
        out_specs=(VMEM,) * 2,
        scratch_shapes=[pltpu.VMEM((4 * HALF, pixels), f32)],
        compiler_params=asked,
        name="masks",
    )(joined_rows((grads, skin, node_refs)))
    spread, *pieces = lax.optimization_barrier((spread, *pieces))
    mine = [pieces[0]]
    for distance in range(1, cams):
        turn = [(c, (c + distance) % cams) for c in range(cams)]
        mine.append(lax.ppermute(pieces[distance], "cams", turn))
    gathered, spread, sums, *mine = lax.optimization_barrier((gathered, spread, sums, *mine))
    table, frames, frame_sums = pl.pallas_call(
        functools.partial(table_kernel, sizes),
        out_shape=(array(side), array(cams * piece), array(8)),
        in_specs=[VMEM],
        out_specs=(VMEM,) * 3,
        compiler_params=asked,
        name="table",
    )(gathered)
    other = lax.ppermute(table, "cams", [(c, c ^ 1) for c in range(cams)])
    pulled = pl.pallas_call(
        own_kernel,
        out_shape=jax.ShapeDtypeStruct((lanes, pixels), f32),
        in_specs=[VMEM] * 2,
        out_specs=VMEM,
        compiler_params=asked,
        name="own_half",
    )(table, masked)
    products = pl.pallas_call(
        functools.partial(data_kernel, sizes),
        out_shape=array(devices * back_rows),
        in_specs=[VMEM] * 6,
        out_specs=VMEM,
        scratch_shapes=[pltpu.VMEM((2 * side, lanes), f32)],
        compiler_params=asked,
        name="data_products",
    )(pulled, other, sums, frame_sums, spread, masked)
    received = exchange(products, AXES)

    scalars, blocks = pl.pallas_call(
        functools.partial(image_kernel, sizes),
        out_shape=(array(8), array(devices * (piece + 1))),
        in_specs=[VMEM] * (3 + cams),
        out_specs=(VMEM,) * 2,
        scratch_shapes=[pltpu.VMEM((cams * piece, lanes), f32)],
        compiler_params=asked,
        name="image",
    )(choose, received, frames, *mine)
    arrived = exchange(blocks, AXES)
    outs = pl.pallas_call(
        functools.partial(update_kernel, sizes),
        out_shape=(array(rows),) * 3,
        in_specs=[VMEM] * 6,
        out_specs=(VMEM,) * 3,
        compiler_params=asked,
        name="update",
    )(arrived, scalars, iterate, residual, direction, precond)
    return tuple(jnp.transpose(v.reshape(params, held, lanes), (1, 0, 2)) for v in outs)


def solution(mesh):
    split = P(AXES, None, None)
    pixel_split = P(None, AXES)
    in_specs = (split,) * 4 + (P("nodes", None, None),) + (pixel_split,) * 3 + (split,)
    return jax.shard_map(
        on_device, mesh=mesh, in_specs=in_specs, out_specs=(split,) * 3, check_vma=False
    )
```

profile of v0, /device:TPU:0, one launch (start us, length us, event | category | flops | bytes accessed | tf_op | source)
XLA Modules:
  0.0 46.8 jit_solution(16823080569094798934)
XLA Ops:
  0.6 0.7 %convert_add_fusion.2 = f32[32,1,128]{2,1,0:T(1,128)S(1)} fusion(s32[3,1,8]{2,1,0:T(1,128)} %bitcast.48, f32[24,1,128]{2,1,0:T(1,128)} %bitcast.39), kind=kLoop, calls=%fused_computation.2 | loop fusion | flops 8192 | bytes 28768 | tf_op jit(solution)/shard_map/add | solution.py:356
  1.4 0.8 %pack.1 = f32[416,128]{1,0:T(8,128)} custom-call(f32[32,128]{1,0:T(8,128)S(1)} %bitcast.42), custom_call_target="tpu_custom_call" | custom-call | tf_op jit(solution)/shard_map/pack/pallas_call | solution.py:396
  2.1 7.3 %all-to-all-start = ((f32[32,13,1,128]{3,2,1,0:T(1,128)}), f32[32,13,1,128]{3,2,1,0:T(1,128)S(1)}, u32[]{:S(2)}, u32[]{:S(2)}) async-start(f32[32,13,1,128]{3,2,1,0:T(1,128)} %bitcast.8), calls=%async_computation | async-start | bytes 425984 | tf_op jit(solution)/shard_map/all_to_all | solution.py:365
  9.4 0.8 %convert_add_fusion.1 = f32[48,2,128]{2,1,0:T(2,128)S(1)} fusion(s32[6,2,128]{2,1,0:T(2,128)} %bitcast.50, f32[12,2,128]{2,1,0:T(2,128)} %bitcast.43, f32[12,2,128]{2,1,0:T(2,128)} %bitcast.45, f32[12,2,128]{2,1,0:T(2,128)} %bitcast.40), kind=kLoop, calls=%fused_computation.1 | loop fusion | flops 49152 | bytes 92160 | tf_op jit(solution)/shard_map/add | solution.py:356
  10.2 0.0 copy-start.4
  10.2 0.7 %copy-done.4 = s32[1,8,3]{1,0,2:T(1,128)S(1)} copy-done((s32[1,8,3]{1,0,2:T(1,128)S(1)}, s32[1,8,3]{1,0,2:T(1,128)}, u32[]{:S(2)}) %copy-start.4) | copy-done | bytes 120
  10.9 0.8 %near.1 = (f32[8,128]{1,0:T(8,128)S(1)}, bf16[32,320]{1,0:T(8,128)(2,1)S(1)}, f32[18,128]{1,0:T(8,128)S(1)}, f32[18,128]{1,0:T(8,128)S(1)}, f32[18,128]{1,0:T(8,128)S(1)}, /*index=5*/f32[18,128]{1,0:T(8,128)S(1)}) custom-call(s32[3,1,8]{2,1,0:T(1,128)S(1)} %bitcast.49, f32[96,128]{1,0:T(8,128)S(1)} %bitcast.37), custom_call_target="tpu_custom_call" | custom-call | tf_op jit(solution)/shard_map/near/pallas_call | solution.py:418
  11.7 0.9 %convert_add_fusion.pixel_rows = f32[24,2048]{1,0:T(8,128)S(1)} fusion(s32[4,2048]{1,0:T(4,128)} %param.15, bf16[4,2048]{1,0:T(4,128)(2,1)} %param.16, bf16[12,2048]{1,0:T(8,128)(2,1)} %param.14), kind=kLoop, calls=%fused_computation | loop fusion | flops 245760 | bytes 294912 | tf_op jit(solution)/shard_map/add | solution.py:356
  12.7 1.1 %masks.1 = (f32[128,2048]{1,0:T(8,128)S(1)}, bf16[384,2048]{1,0:T(8,128)(2,1)S(1)}) custom-call(f32[24,2048]{1,0:T(8,128)S(1)} %convert_add_fusion.pixel_rows), custom_call_target="tpu_custom_call" | custom-call | tf_op jit(solution)/shard_map/masks/pallas_call | solution.py:428
  13.8 0.3 collective-permute-start
  14.1 1.7 %collective-permute-start.1 = (f32[18,128]{1,0:T(8,128)S(1)}, f32[18,128]{1,0:T(8,128)S(1)}, u32[]{:S(2)}, u32[]{:S(2)}) collective-permute-start(f32[18,128]{1,0:T(8,128)S(1)} %get-tuple-element.47), channel_id=1, source_target_pairs={{0,2},{1,3},{2,0},{3,1},{4,6},{5,7},{6,4},{7,5},{8,10},{9,11},{10,... | collective-permute-start | bytes 27656 | tf_op jit(solution)/shard_map/ppermute | solution.py:444
  15.8 1.3 %collective-permute-start.2 = (f32[18,128]{1,0:T(8,128)S(1)}, f32[18,128]{1,0:T(8,128)S(1)}, u32[]{:S(2)}, u32[]{:S(2)}) collective-permute-start(f32[18,128]{1,0:T(8,128)S(1)} %get-tuple-element.48), channel_id=1, source_target_pairs={{0,3},{1,0},{2,1},{3,2},{4,7},{5,4},{6,5},{7,6},{8,11},{9,8},{10,9... | collective-permute-start | bytes 27656 | tf_op jit(solution)/shard_map/ppermute | solution.py:444
  17.1 0.0 collective-permute-done.refs_1_
  17.1 0.7 %collective-permute-done.1.refs_2_ = f32[18,128]{1,0:T(8,128)S(1)} collective-permute-done((f32[18,128]{1,0:T(8,128)S(1)}, f32[18,128]{1,0:T(8,128)S(1)}, u32[]{:S(2)}, u32[]{:S(2)}) %collective-permute-start.1) | collective-permute-done | bytes 9248 | tf_op jit(solution)/shard_map/ppermute | solution.py:444
  17.8 0.7 %collective-permute-done.2.refs_3_ = f32[18,128]{1,0:T(8,128)S(1)} collective-permute-done((f32[18,128]{1,0:T(8,128)S(1)}, f32[18,128]{1,0:T(8,128)S(1)}, u32[]{:S(2)}, u32[]{:S(2)}) %collective-permute-start.2) | collective-permute-done | bytes 9248 | tf_op jit(solution)/shard_map/ppermute | solution.py:444
  18.5 0.3 all-to-all-done
  18.8 0.3 table.1
  19.2 0.4 collective-permute-start.3
  19.5 0.5 own_half.1.pulled_own
  20.0 0.5 %collective-permute-done.3.table = f32[192,128]{1,0:T(8,128)S(1)} collective-permute-done((f32[192,128]{1,0:T(8,128)S(1)}, f32[192,128]{1,0:T(8,128)S(1)}, u32[]{:S(2)}, u32[]{:S(2)}) %collective-permute-start.3) | collective-permute-done | bytes 98336 | tf_op jit(solution)/shard_map/ppermute | solution.py:454
  20.5 0.0 copy-start
  20.5 0.0 copy-start.1
  20.5 0.0 copy-start.2
  20.5 0.0 copy-start.3
  20.5 1.3 %data_products.1 = f32[320,128]{1,0:T(8,128)S(1)} custom-call(f32[128,2048]{1,0:T(8,128)S(1)} %own_half.1.pulled_own, f32[192,128]{1,0:T(8,128)S(1)} %collective-permute-done.3.table, f32[8,128]{1,0:T(8,128)S(1)} %get-tuple-element.52.near_sums, f32[8,128]{1,0:T(8,128)S(1)} %get-tuple-element.53.frame_sums, f32[128,2048]{1,0:T(8,128)S(1)} %get-tuple-element.54.spread, ...), custom_call_target="tpu_custom_call" | custom-call | tf_op jit(solution)/shard_map/data_products/pallas_call | solution.py:463
  21.8 13.9 %all_to_all.15 = f32[32,10,1,128]{3,2,1,0:T(1,128)S(1)} all-to-all(f32[32,10,1,128]{3,2,1,0:T(1,128)S(1)} %bitcast.35), channel_id=1, replica_groups=mesh['nodes'=8,'cams'=4] {'nodes','cams'}, dimensions={0} | all-to-all | bytes 327680 | tf_op jit(solution)/shard_map/all_to_all | solution.py:365
  35.7 0.3 image.1
  35.9 10.2 %all_to_all.16 = f32[32,7,1,128]{3,2,1,0:T(1,128)S(1)} all-to-all(f32[32,7,1,128]{3,2,1,0:T(1,128)S(1)} %bitcast.38), channel_id=1, replica_groups=mesh['nodes'=8,'cams'=4] {'nodes','cams'}, dimensions={0} | all-to-all | bytes 229376 | tf_op jit(solution)/shard_map/all_to_all | solution.py:365
  46.1 0.0 copy-done
  46.1 0.0 copy-done.1
  46.1 0.0 copy-done.2
  46.1 0.0 copy-done.3
  46.1 0.7 %update.1 = (f32[24,128]{1,0:T(8,128)}, f32[24,128]{1,0:T(8,128)}, f32[24,128]{1,0:T(8,128)}) custom-call(f32[224,128]{1,0:T(8,128)S(1)} %bitcast.36, f32[8,128]{1,0:T(8,128)S(1)} %get-tuple-element.61.scalars, f32[24,128]{1,0:T(8,128)S(1)} %bitcast.47, f32[24,128]{1,0:T(8,128)S(1)} %bitcast.46, f32[24,128]{1,0:T(8,128)S(1)} %bitcast.41, f32[24,128]{1,0:T(8,128)S(1)} %bitcast.44), custom_call_target="tpu_custom_call" | custom-call | tf_op jit(solution)/shard_map/update/pallas_call | solution.py:484
Async XLA Ops:
  2.1 16.7 %all-to-all-start = ((f32[32,13,1,128]{3,2,1,0:T(1,128)}), f32[32,13,1,128]{3,2,1,0:T(1,128)S(1)}, u32[]{:S(2)}, u32[]{:S(2)}) async-start(f32[32,13,1,128]{3,2,1,0:T(1,128)} %bitcast.8), calls=%async_computation | async-start | bytes 425984 | tf_op jit(solution)/shard_map/all_to_all | solution.py:365
  10.2 0.7 %copy-start.4 = (s32[1,8,3]{1,0,2:T(1,128)S(1)}, s32[1,8,3]{1,0,2:T(1,128)}, u32[]{:S(2)}) copy-start(s32[1,8,3]{1,0,2:T(1,128)} %param.13) | copy-start | bytes 292
  13.8 3.3 %collective-permute-start = (f32[18,128]{1,0:T(8,128)S(1)}, f32[18,128]{1,0:T(8,128)S(1)}, u32[]{:S(2)}, u32[]{:S(2)}) collective-permute-start(f32[18,128]{1,0:T(8,128)S(1)} %get-tuple-element.46), channel_id=1, source_target_pairs={{0,1},{1,2},{2,3},{3,0},{4,5},{5,6},{6,7},{7,4},{8,9},{9,10},{10,1... | collective-permute-start | bytes 27656 | tf_op jit(solution)/shard_map/ppermute | solution.py:444
  14.1 3.7 %collective-permute-start.1 = (f32[18,128]{1,0:T(8,128)S(1)}, f32[18,128]{1,0:T(8,128)S(1)}, u32[]{:S(2)}, u32[]{:S(2)}) collective-permute-start(f32[18,128]{1,0:T(8,128)S(1)} %get-tuple-element.47), channel_id=1, source_target_pairs={{0,2},{1,3},{2,0},{3,1},{4,6},{5,7},{6,4},{7,5},{8,10},{9,11},{10,... | collective-permute-start | bytes 27656 | tf_op jit(solution)/shard_map/ppermute | solution.py:444
  15.8 2.7 %collective-permute-start.2 = (f32[18,128]{1,0:T(8,128)S(1)}, f32[18,128]{1,0:T(8,128)S(1)}, u32[]{:S(2)}, u32[]{:S(2)}) collective-permute-start(f32[18,128]{1,0:T(8,128)S(1)} %get-tuple-element.48), channel_id=1, source_target_pairs={{0,3},{1,0},{2,1},{3,2},{4,7},{5,4},{6,5},{7,6},{8,11},{9,8},{10,9... | collective-permute-start | bytes 27656 | tf_op jit(solution)/shard_map/ppermute | solution.py:444
  19.2 1.3 %collective-permute-start.3 = (f32[192,128]{1,0:T(8,128)S(1)}, f32[192,128]{1,0:T(8,128)S(1)}, u32[]{:S(2)}, u32[]{:S(2)}) collective-permute-start(f32[192,128]{1,0:T(8,128)S(1)} %get-tuple-element.50.table), channel_id=1, source_target_pairs={{0,1},{1,0},{2,3},{3,2},{4,5},{5,4},{6,7},{7,6},{8,9},{9,8},{10,11... | collective-permute-start | bytes 294920 | tf_op jit(solution)/shard_map/ppermute | solution.py:454
  20.5 25.6 %copy-start = (f32[2,12,128]{2,0,1:T(2,128)S(1)}, f32[2,12,128]{2,0,1:T(2,128)}, u32[]{:S(2)}) copy-start(f32[2,12,128]{2,0,1:T(2,128)} %param.11) | copy-start | bytes 36868
  20.5 25.6 %copy-start.1 = (f32[2,12,128]{2,0,1:T(2,128)S(1)}, f32[2,12,128]{2,0,1:T(2,128)}, u32[]{:S(2)}) copy-start(f32[2,12,128]{2,0,1:T(2,128)} %param.12) | copy-start | bytes 36868
  20.5 25.6 %copy-start.2 = (f32[2,12,128]{2,0,1:T(2,128)S(1)}, f32[2,12,128]{2,0,1:T(2,128)}, u32[]{:S(2)}) copy-start(f32[2,12,128]{2,0,1:T(2,128)} %param.10) | copy-start | bytes 36868
  20.5 25.6 %copy-start.3 = (f32[2,12,128]{2,0,1:T(2,128)S(1)}, f32[2,12,128]{2,0,1:T(2,128)}, u32[]{:S(2)}) copy-start(f32[2,12,128]{2,0,1:T(2,128)} %param.9) | copy-start | bytes 36868
where the time goes:
time: 47.3 us; the launch traced here: 46.8 us
  blocking collectives  24 us (51%)
  starting transfers between devices  11 us (23%)
  Pallas kernels  5.82 us (12%)
  other arithmetic  2.41 us (5%)
  waiting for transfers between devices  2.17 us (5%)
  between operations  0.7 us (1%)
  local copies, waits for them, and re-layouts  0.69 us (1%)
    all_to_all x2, blocking collectives, exchange(): lax.all_to_all(blocks, axes, split_axis=0, concat_axis=0, tiled=True)  24 us
    all_to_all x1, starting transfers between devices, exchange(): lax.all_to_all(blocks, axes, split_axis=0, concat_axis=0, tiled=True)  7.3 us
    ppermute x3, starting transfers between devices, on_device(): mine.append(lax.ppermute(pieces[distance], 'cams', turn))  3.3 us
    add x3, other arithmetic, joined_rows(): total = value if total is None else total + value  2.41 us
    ppermute x3, waiting for transfers between devices, on_device(): mine.append(lax.ppermute(pieces[distance], 'cams', turn))  1.4 us
    pallas_call x1, Pallas kernels, on_device(): pl.pallas_call(functools.partial(data_kernel, sizes), out_shape=array(dev...  1.25 us
    pallas_call x1, Pallas kernels, on_device(): pl.pallas_call(functools.partial(masks_kernel, params, node_refs.shape[0]...  1.15 us
  transfers between devices with their start and end apart: 5, of which 4 were waited for; matrix products, arithmetic and copies ran while one was open for 4% of the time, Pallas kernels for 5%

commit v1 on v0

--- a/solution.py
+++ b/solution.py
@@ -114,14 +114,12 @@
     column = lax.broadcasted_iota(jnp.int32, (1, choose.shape[1]), 1)
     row = column % back_rows
     slot = column // (back_rows * cams) * slot_count + row // part
-    slot = jnp.where(row < slot_count * part, slot, -1)
     listed = jnp.zeros_like(column)
     for owner in range(owners):
         for s in range(slot_count):
             patch = jnp.maximum(send_list[s, 0, owner], 0)
             listed = jnp.where(slot == owner * slot_count + s, patch, listed)
     target = listed // held * piece + row % part * held + listed % held
-    target = jnp.where(slot >= 0, target, cams * piece)
     image_row = lax.broadcasted_iota(jnp.int32, choose.shape, 0)
     choose[...] = jnp.where(image_row == target, 1.0, 0.0).astype(bf16)
 
@@ -234,12 +232,12 @@
         pulled_out[:, cols] = pull(turned_table, masked, parity, cols)
 
 
-def data_kernel(sizes, pulled_own, table, near_sums, frame_sums, spread, masked, out, products):
+def data_kernel(sizes, pulled_own, table, spread, masked, out, squares_out, products):
     owners, cams, slot_count, held, params, part, half_pieces, extra, back_rows, step = sizes
     side = masked.shape[0] // 2
     parity = 1 - lax.rem(lax.axis_index("cams"), 2)
     turned_table = turned_halves(table)
-    curvature = near_sums[1:2, :] + frame_sums[0:1, :]
+    squares = jnp.zeros((1, LANES), f32)
     chunk = 512
     for at in range(0, spread.shape[1], chunk):
         cols = slice(at, at + chunk)
@@ -248,7 +246,7 @@
         projected = rows_sum(weights * pulled)
         squared = projected * projected
         for lane in range(0, chunk, LANES):
-            curvature = curvature + squared[:, lane : lane + LANES]
+            squares = squares + squared[:, lane : lane + LANES]
         both = jnp.concatenate(halves(weights * projected), axis=0)
         back = lax.dot_general(masked[:, cols], both, NT, preferred_element_type=f32)
         back = back[:, :LANES] + back[:, LANES:]
@@ -257,12 +255,7 @@
         else:
             products[...] += back
 
-    middle = LANES // 2
-    lane_of = lax.broadcasted_iota(jnp.int32, (1, LANES), 1)
-    start = near_sums[0:1, :]
-    start = start + pltpu.roll(start, middle, 1)
-    curvature = curvature + pltpu.roll(curvature, middle, 1)
-    scalars = jnp.where(lane_of < middle, start, curvature)
+    squares_out[0:1, :] = squares
 
     def give(owner):
         for c in range(cams):
@@ -274,14 +267,13 @@
                 else:
                     value = jnp.zeros((part, LANES), f32)
                 out[pl.ds(base + s * part, part), :] = value
-            out[pl.ds(base + slot_count * part, 1), :] = scalars
 
     loop(owners, give)
 
 
-def image_kernel(sizes, choose, received, frames, *refs):
+def image_kernel(sizes, choose, received, frames, near_sums, frame_sums, squares, *refs):
     owners, cams, slot_count, held, params, part, half_pieces, extra, back_rows, step = sizes
-    mine, (scalars, blocks, image) = refs[:cams], refs[cams:]
+    mine, (blocks, image) = refs[:cams], refs[cams:]
     cam = lax.axis_index("cams")
     piece = held * part
     value = received[...]
@@ -291,46 +283,49 @@
         lax.dot_general(choose[...], term, NN, preferred_element_type=f32)
         for term in (high, rest, low)
     )
-    image[...] = total[0 : cams * piece]
-    last = total[cams * piece : cams * piece + 1]
-    half = LANES // 2
-    lane_of = lax.broadcasted_iota(jnp.int32, (1, LANES), 1)
-    start = jnp.sum(jnp.where(lane_of < half, last, 0.0), axis=1, keepdims=True)
-    curvature = jnp.sum(jnp.where(lane_of < half, 0.0, last), axis=1, keepdims=True)
-    length = start / curvature
-    norms = jnp.zeros((1, LANES), f32)
+    image[...] = total[0 : cams * piece] + frames[...]
+    cross = jnp.zeros((1, LANES), f32)
+    square = jnp.zeros((1, LANES), f32)
     for distance, block in enumerate(mine):
         rows = pl.ds(lax.rem(cam + cams - distance, cams) * piece, piece)
         residual, precond, near = (block[k * piece : (k + 1) * piece, :] for k in range(3))
-        value = image[rows, :] + near + frames[rows, :]
+        value = image[rows, :] + near
         image[rows, :] = value
-        left = residual - length * value
-        norms = norms + rows_sum(left * (precond * left))
-    scalars[0:1, :] = jnp.broadcast_to(start, (1, LANES))
-    scalars[1:2, :] = jnp.broadcast_to(length, (1, LANES))
+        cross = cross + rows_sum(value * (precond * residual))
+        square = square + rows_sum(value * (precond * value))
+    curvature = near_sums[1:2, :] + frame_sums[0:1, :] + squares[0:1, :]
+    lane_of = lax.broadcasted_iota(jnp.int32, (1, LANES), 1)
+    scalars = jnp.zeros((1, LANES), f32)
+    for k, row in enumerate((near_sums[0:1, :], curvature, cross, square)):
+        scalars = jnp.where(lane_of == k, jnp.sum(row, axis=1, keepdims=True), scalars)
 
     def tell(owner):
         for c in range(cams):
             base = (owner * cams + c) * (piece + 1)
-            blocks[pl.ds(base, 1), :] = norms
+            blocks[pl.ds(base, 1), :] = scalars
             blocks[pl.ds(base + 1, piece), :] = image[c * piece : (c + 1) * piece, :]
 
     loop(owners, tell)
 
 
 def update_kernel(
-    sizes, arrived, scalars, iterate, residual, direction, precond,
+    sizes, arrived, iterate, residual, direction, precond,
     new_iterate, new_residual, new_direction,
 ):
     owners, cams, slot_count, held, params, part, half_pieces, extra, back_rows, step = sizes
     piece = held * part
     rows = iterate.shape[0]
     own = lax.axis_index("nodes")
-    norms = arrived[0:1, :]
+    scalars = arrived[0:1, :]
     for device in range(1, owners * cams):
-        norms = norms + arrived[device * (piece + 1) : device * (piece + 1) + 1, :]
-    start, length = scalars[0:1, :], scalars[1:2, :]
-    ratio = jnp.sum(norms, axis=1, keepdims=True) / start
+        scalars = scalars + arrived[device * (piece + 1) : device * (piece + 1) + 1, :]
+    lane_of = lax.broadcasted_iota(jnp.int32, (1, LANES), 1)
+    start, curvature, cross, square = (
+        jnp.sum(jnp.where(lane_of == k, scalars, 0.0), axis=1, keepdims=True) for k in range(4)
+    )
+    length = start / curvature
+    norm = start - 2.0 * length * cross + length * length * square
+    ratio = norm / start
     for c in range(rows // piece):
         here = slice(c * piece, (c + 1) * piece)
         image = arrived[pl.ds((own * cams + c) * (piece + 1) + 1, piece), :]
@@ -379,7 +374,7 @@
     extra = -(-slots // lanes)
     part = next(n for n in range(1, params + 1) if params % n == 0 and n * cams >= params)
     piece = held * part
-    back_rows = slot_count * part + 1
+    back_rows = slot_count * part
     half_pieces = -(-(params // part) // 2)
     side = (slots + slots % 2) * HALF
     sizes = (
@@ -414,7 +409,7 @@
         [v.reshape(params, held, lanes) for v in (direction, residual, precond)]
         + [jnp.transpose(rigid_nbr, (1, 0, 2))]
     ).reshape(-1, lanes)
-    image_rows = -(-(cams * piece + 1) // 16) * 16
+    image_rows = -(-cams * piece // 16) * 16
     sums, choose, *pieces = pl.pallas_call(
         functools.partial(near_kernel, sizes, rows, rigid_nbr.shape[1]),
         out_shape=(array(8), jax.ShapeDtypeStruct((image_rows, devices * back_rows), bf16))
@@ -437,12 +432,7 @@
         compiler_params=asked,
         name="masks",
     )(joined_rows((grads, skin, node_refs)))
-    spread, *pieces = lax.optimization_barrier((spread, *pieces))
-    mine = [pieces[0]]
-    for distance in range(1, cams):
-        turn = [(c, (c + distance) % cams) for c in range(cams)]
-        mine.append(lax.ppermute(pieces[distance], "cams", turn))
-    gathered, spread, sums, *mine = lax.optimization_barrier((gathered, spread, sums, *mine))
+    gathered, spread, sums = lax.optimization_barrier((gathered, spread, sums))
     table, frames, frame_sums = pl.pallas_call(
         functools.partial(table_kernel, sizes),
         out_shape=(array(side), array(cams * piece), array(8)),
@@ -460,35 +450,40 @@
         compiler_params=asked,
         name="own_half",
     )(table, masked)
-    products = pl.pallas_call(
+    products, squares = pl.pallas_call(
         functools.partial(data_kernel, sizes),
-        out_shape=array(devices * back_rows),
-        in_specs=[VMEM] * 6,
+        out_shape=(array(devices * back_rows), array(8)),
+        in_specs=[VMEM] * 4,
+        out_specs=(VMEM,) * 2,
+        scratch_shapes=[pltpu.VMEM((2 * side, lanes), f32)],
+        compiler_params=asked,
+        name="data_products",
+    )(pulled, other, spread, masked)
+    products, *pieces = lax.optimization_barrier((products, *pieces))
+    received = exchange(products, AXES)
+    mine = [pieces[0]]
+    for distance in range(1, cams):
+        turn = [(c, (c + distance) % cams) for c in range(cams)]
+        mine.append(lax.ppermute(pieces[distance], "cams", turn))
+
+    blocks = pl.pallas_call(
+        functools.partial(image_kernel, sizes),
+        out_shape=array(devices * (piece + 1)),
+        in_specs=[VMEM] * (6 + cams),
         out_specs=VMEM,
-        scratch_shapes=[pltpu.VMEM((2 * side, lanes), f32)],
-        compiler_params=asked,
-        name="data_products",
-    )(pulled, other, sums, frame_sums, spread, masked)
-    received = exchange(products, AXES)
-
-    scalars, blocks = pl.pallas_call(
-        functools.partial(image_kernel, sizes),
-        out_shape=(array(8), array(devices * (piece + 1))),
-        in_specs=[VMEM] * (3 + cams),
-        out_specs=(VMEM,) * 2,
         scratch_shapes=[pltpu.VMEM((cams * piece, lanes), f32)],
         compiler_params=asked,
         name="image",
-    )(choose, received, frames, *mine)
+    )(choose, received, frames, sums, frame_sums, squares, *mine)
     arrived = exchange(blocks, AXES)
     outs = pl.pallas_call(
         functools.partial(update_kernel, sizes),
         out_shape=(array(rows),) * 3,
-        in_specs=[VMEM] * 6,
+        in_specs=[VMEM] * 5,
         out_specs=(VMEM,) * 3,
         compiler_params=asked,
         name="update",
-    )(arrived, scalars, iterate, residual, direction, precond)
+    )(arrived, iterate, residual, direction, precond)
     return tuple(jnp.transpose(v.reshape(params, held, lanes), (1, 0, 2)) for v in outs)
 
 

time: 47.3 us -> 44.9 us (0.949)
  blocking collectives: 24 us -> 9.95 us
  waiting for transfers between devices: 2.17 us -> 10.5 us
  starting transfers between devices: 11 us -> 13.6 us
  Pallas kernels: 5.82 us -> 6.52 us
    all_to_all x2 -> x1, blocking collectives: 24 us -> 9.95 us  [exchange(): lax.all_to_all(blocks, axes, split_axis=0, concat_axis=0, tiled=True)]
    all_to_all x1 -> x2, waiting for transfers between devices: 0.3 us -> 8.71 us  [exchange(): lax.all_to_all(blocks, axes, split_axis=0, concat_axis=0, tiled=True)]
    all_to_all x1 -> x2, starting transfers between devices: 7.3 us -> 9.88 us  [exchange(): lax.all_to_all(blocks, axes, split_axis=0, concat_axis=0, tiled=True)]
    pallas_call x2, Pallas kernels: 1.52 us -> 2.2 us  [the longest x1 1.92 us: on_device(): pl.pallas_call(functools.partial(data_kernel, sizes), out_shape=(array(de...]
  transfers between devices with their start and end apart: 5 -> 6, of which waited for: 4 -> 5; matrix products, arithmetic and copies ran while one was open for 4% -> 4% of each run, Pallas kernels for 5% -> 6%
where the time goes in v1:
time: 44.9 us; the launch traced here: 44.4 us
  starting transfers between devices  13.6 us (30%)
  waiting for transfers between devices  10.5 us (23%)
  blocking collectives  9.95 us (22%)
  Pallas kernels  6.52 us (15%)
  other arithmetic  2.41 us (5%)
  between operations  0.73 us (2%)
  local copies, waits for them, and re-layouts  0.7 us (2%)
    all_to_all x1, blocking collectives, exchange(): lax.all_to_all(blocks, axes, split_axis=0, concat_axis=0, tiled=True)  9.95 us
    all_to_all x2, starting transfers between devices, exchange(): lax.all_to_all(blocks, axes, split_axis=0, concat_axis=0, tiled=True)  9.88 us
    all_to_all x2, waiting for transfers between devices, exchange(): lax.all_to_all(blocks, axes, split_axis=0, concat_axis=0, tiled=True)  8.71 us
    ppermute x3, starting transfers between devices, on_device(): mine.append(lax.ppermute(pieces[distance], 'cams', turn))  3.3 us
    add x3, other arithmetic, joined_rows(): total = value if total is None else total + value  2.41 us
    pallas_call x1, Pallas kernels, on_device(): pl.pallas_call(functools.partial(data_kernel, sizes), out_shape=(array(de...  1.92 us
    ppermute x3, waiting for transfers between devices, on_device(): mine.append(lax.ppermute(pieces[distance], 'cams', turn))  1.4 us
    pallas_call x1, Pallas kernels, on_device(): pl.pallas_call(functools.partial(masks_kernel, params, node_refs.shape[0]...  1.15 us
  transfers between devices with their start and end apart: 6, of which 5 were waited for; matrix products, arithmetic and copies ran while one was open for 4% of the time, Pallas kernels for 6%

profile of v1, /device:TPU:0, one launch (start us, length us, event | category | flops | bytes accessed | tf_op | source)
XLA Modules:
  0.0 44.4 jit_solution(5313638694020918435)
XLA Ops:
  0.6 0.7 %convert_add_fusion.2 = f32[32,1,128]{2,1,0:T(1,128)S(1)} fusion(s32[3,1,8]{2,1,0:T(1,128)} %bitcast.47, f32[24,1,128]{2,1,0:T(1,128)} %bitcast.38), kind=kLoop, calls=%fused_computation.2 | loop fusion | flops 8192 | bytes 28768 | tf_op jit(solution)/shard_map/add | solution.py:351
  1.4 0.8 %pack.1 = f32[416,128]{1,0:T(8,128)} custom-call(f32[32,128]{1,0:T(8,128)S(1)} %bitcast.41), custom_call_target="tpu_custom_call" | custom-call | tf_op jit(solution)/shard_map/pack/pallas_call | solution.py:391
  2.1 7.3 %all-to-all-start = ((f32[32,13,1,128]{3,2,1,0:T(1,128)}), f32[32,13,1,128]{3,2,1,0:T(1,128)S(1)}, u32[]{:S(2)}, u32[]{:S(2)}) async-start(f32[32,13,1,128]{3,2,1,0:T(1,128)} %bitcast.8), calls=%async_computation | async-start | bytes 425984 | tf_op jit(solution)/shard_map/all_to_all | solution.py:360
  9.5 0.8 %convert_add_fusion.1 = f32[48,2,128]{2,1,0:T(2,128)S(1)} fusion(s32[6,2,128]{2,1,0:T(2,128)} %bitcast.49, f32[12,2,128]{2,1,0:T(2,128)} %bitcast.42, f32[12,2,128]{2,1,0:T(2,128)} %bitcast.44, f32[12,2,128]{2,1,0:T(2,128)} %bitcast.39), kind=kLoop, calls=%fused_computation.1 | loop fusion | flops 49152 | bytes 92160 | tf_op jit(solution)/shard_map/add | solution.py:351
  10.2 0.0 copy-start.4
  10.2 0.7 %copy-done.4 = s32[1,8,3]{1,0,2:T(1,128)S(1)} copy-done((s32[1,8,3]{1,0,2:T(1,128)S(1)}, s32[1,8,3]{1,0,2:T(1,128)}, u32[]{:S(2)}) %copy-start.4) | copy-done | bytes 120
  10.9 0.8 %near.1 = (f32[8,128]{1,0:T(8,128)S(1)}, bf16[32,288]{1,0:T(8,128)(2,1)S(1)}, f32[18,128]{1,0:T(8,128)S(1)}, f32[18,128]{1,0:T(8,128)S(1)}, f32[18,128]{1,0:T(8,128)S(1)}, /*index=5*/f32[18,128]{1,0:T(8,128)S(1)}) custom-call(s32[3,1,8]{2,1,0:T(1,128)S(1)} %bitcast.48, f32[96,128]{1,0:T(8,128)S(1)} %bitcast.37), custom_call_target="tpu_custom_call" | custom-call | tf_op jit(solution)/shard_map/near/pallas_call | solution.py:413
  11.8 0.9 %convert_add_fusion.pixel_rows = f32[24,2048]{1,0:T(8,128)S(1)} fusion(s32[4,2048]{1,0:T(4,128)} %param.15, bf16[4,2048]{1,0:T(4,128)(2,1)} %param.16, bf16[12,2048]{1,0:T(8,128)(2,1)} %param.14), kind=kLoop, calls=%fused_computation | loop fusion | flops 245760 | bytes 294912 | tf_op jit(solution)/shard_map/add | solution.py:351
  12.7 1.1 %masks.1 = (f32[128,2048]{1,0:T(8,128)S(1)}, bf16[384,2048]{1,0:T(8,128)(2,1)S(1)}) custom-call(f32[24,2048]{1,0:T(8,128)S(1)} %convert_add_fusion.pixel_rows), custom_call_target="tpu_custom_call" | custom-call | tf_op jit(solution)/shard_map/masks/pallas_call | solution.py:423
  13.8 5.0 %all-to-all-done = f32[32,13,1,128]{3,2,1,0:T(1,128)S(1)} async-done(((f32[32,13,1,128]{3,2,1,0:T(1,128)}), f32[32,13,1,128]{3,2,1,0:T(1,128)S(1)}, u32[]{:S(2)}, u32[]{:S(2)}) %all-to-all-start) | async-done | bytes 213024 | tf_op jit(solution)/shard_map/all_to_all | solution.py:360
  18.8 0.3 table.1
  19.2 0.4 collective-permute-start
  19.6 0.5 %own_half.1.pulled_own = f32[128,2048]{1,0:T(8,128)S(1)} custom-call(f32[192,128]{1,0:T(8,128)S(1)} %get-tuple-element.37.table, bf16[384,2048]{1,0:T(8,128)(2,1)S(1)} %get-tuple-element.38.masked), custom_call_target="tpu_custom_call" | custom-call | tf_op jit(solution)/shard_map/own_half/pallas_call | solution.py:445
  20.0 0.0 copy-start
  20.0 0.0 copy-start.1
  20.1 0.0 copy-start.2
  20.1 0.0 copy-start.3
  20.1 0.4 collective-permute-done.table
  20.5 1.9 %data_products.1 = (f32[288,128]{1,0:T(8,128)}, f32[8,128]{1,0:T(8,128)S(1)}) custom-call(f32[128,2048]{1,0:T(8,128)S(1)} %own_half.1.pulled_own, f32[192,128]{1,0:T(8,128)S(1)} %collective-permute-done.table, f32[128,2048]{1,0:T(8,128)S(1)} %get-tuple-element.39.spread, bf16[384,2048]{1,0:T(8,128)(2,1)S(1)} %get-tuple-element.38.masked), custom_call_target="tpu_custom_call" | custom-call | tf_op jit(solution)/shard_map/data_products/pallas_call | solution.py:453
  22.4 2.6 %all-to-all-start.1 = ((f32[32,9,1,128]{3,2,1,0:T(1,128)}), f32[32,9,1,128]{3,2,1,0:T(1,128)S(1)}, u32[]{:S(2)}, u32[]{:S(2)}) async-start(f32[32,9,1,128]{3,2,1,0:T(1,128)} %bitcast.10), calls=%async_computation.1 | async-start | bytes 294912 | tf_op jit(solution)/shard_map/all_to_all | solution.py:360
  25.0 0.3 collective-permute-start.1
  25.3 1.7 %collective-permute-start.2 = (f32[18,128]{1,0:T(8,128)S(1)}, f32[18,128]{1,0:T(8,128)S(1)}, u32[]{:S(2)}, u32[]{:S(2)}) collective-permute-start(f32[18,128]{1,0:T(8,128)S(1)} %get-tuple-element.52), channel_id=1, source_target_pairs={{0,2},{1,3},{2,0},{3,1},{4,6},{5,7},{6,4},{7,5},{8,10},{9,11},{10,... | collective-permute-start | bytes 27656 | tf_op jit(solution)/shard_map/ppermute | solution.py:467
  27.0 1.3 %collective-permute-start.3 = (f32[18,128]{1,0:T(8,128)S(1)}, f32[18,128]{1,0:T(8,128)S(1)}, u32[]{:S(2)}, u32[]{:S(2)}) collective-permute-start(f32[18,128]{1,0:T(8,128)S(1)} %get-tuple-element.53), channel_id=1, source_target_pairs={{0,3},{1,0},{2,1},{3,2},{4,7},{5,4},{6,5},{7,6},{8,11},{9,8},{10,9... | collective-permute-start | bytes 27656 | tf_op jit(solution)/shard_map/ppermute | solution.py:467
  28.3 0.0 collective-permute-done.1.refs_1_
  28.3 0.8 %collective-permute-done.2.refs_2_ = f32[18,128]{1,0:T(8,128)S(1)} collective-permute-done((f32[18,128]{1,0:T(8,128)S(1)}, f32[18,128]{1,0:T(8,128)S(1)}, u32[]{:S(2)}, u32[]{:S(2)}) %collective-permute-start.2) | collective-permute-done | bytes 9248 | tf_op jit(solution)/shard_map/ppermute | solution.py:467
  29.1 0.6 %collective-permute-done.3.refs_3_ = f32[18,128]{1,0:T(8,128)S(1)} collective-permute-done((f32[18,128]{1,0:T(8,128)S(1)}, f32[18,128]{1,0:T(8,128)S(1)}, u32[]{:S(2)}, u32[]{:S(2)}) %collective-permute-start.3) | collective-permute-done | bytes 9248 | tf_op jit(solution)/shard_map/ppermute | solution.py:467
  29.7 3.7 %all-to-all-done.1 = f32[32,9,1,128]{3,2,1,0:T(1,128)S(1)} async-done(((f32[32,9,1,128]{3,2,1,0:T(1,128)}), f32[32,9,1,128]{3,2,1,0:T(1,128)S(1)}, u32[]{:S(2)}, u32[]{:S(2)}) %all-to-all-start.1) | async-done | bytes 147488 | tf_op jit(solution)/shard_map/all_to_all | solution.py:360
  33.4 0.3 image.1
  33.7 9.9 %all_to_all.15 = f32[32,7,1,128]{3,2,1,0:T(1,128)S(1)} all-to-all(f32[32,7,1,128]{3,2,1,0:T(1,128)S(1)} %bitcast.36), channel_id=1, replica_groups=mesh['nodes'=8,'cams'=4] {'nodes','cams'}, dimensions={0} | all-to-all | bytes 229376 | tf_op jit(solution)/shard_map/all_to_all | solution.py:360
  43.7 0.0 copy-done
  43.7 0.0 copy-done.1
  43.7 0.0 copy-done.2
  43.7 0.0 copy-done.3
  43.7 0.7 %update.1 = (f32[24,128]{1,0:T(8,128)}, f32[24,128]{1,0:T(8,128)}, f32[24,128]{1,0:T(8,128)}) custom-call(f32[224,128]{1,0:T(8,128)S(1)} %bitcast.35, f32[24,128]{1,0:T(8,128)S(1)} %bitcast.46, f32[24,128]{1,0:T(8,128)S(1)} %bitcast.45, f32[24,128]{1,0:T(8,128)S(1)} %bitcast.40, f32[24,128]{1,0:T(8,128)S(1)} %bitcast.43), custom_call_target="tpu_custom_call" | custom-call | tf_op jit(solution)/shard_map/update/pallas_call | solution.py:479
Async XLA Ops:
  2.1 16.7 %all-to-all-start = ((f32[32,13,1,128]{3,2,1,0:T(1,128)}), f32[32,13,1,128]{3,2,1,0:T(1,128)S(1)}, u32[]{:S(2)}, u32[]{:S(2)}) async-start(f32[32,13,1,128]{3,2,1,0:T(1,128)} %bitcast.8), calls=%async_computation | async-start | bytes 425984 | tf_op jit(solution)/shard_map/all_to_all | solution.py:360
  10.2 0.7 %copy-start.4 = (s32[1,8,3]{1,0,2:T(1,128)S(1)}, s32[1,8,3]{1,0,2:T(1,128)}, u32[]{:S(2)}) copy-start(s32[1,8,3]{1,0,2:T(1,128)} %param.13) | copy-start | bytes 292
  19.2 1.3 %collective-permute-start = (f32[192,128]{1,0:T(8,128)S(1)}, f32[192,128]{1,0:T(8,128)S(1)}, u32[]{:S(2)}, u32[]{:S(2)}) collective-permute-start(f32[192,128]{1,0:T(8,128)S(1)} %get-tuple-element.37.table), channel_id=1, source_target_pairs={{0,1},{1,0},{2,3},{3,2},{4,5},{5,4},{6,7},{7,6},{8,9},{9,8},{10,11... | collective-permute-start | bytes 294920 | tf_op jit(solution)/shard_map/ppermute | solution.py:444
  20.0 23.6 %copy-start = (f32[2,12,128]{2,0,1:T(2,128)S(1)}, f32[2,12,128]{2,0,1:T(2,128)}, u32[]{:S(2)}) copy-start(f32[2,12,128]{2,0,1:T(2,128)} %param.11) | copy-start | bytes 36868
  20.0 23.6 %copy-start.1 = (f32[2,12,128]{2,0,1:T(2,128)S(1)}, f32[2,12,128]{2,0,1:T(2,128)}, u32[]{:S(2)}) copy-start(f32[2,12,128]{2,0,1:T(2,128)} %param.12) | copy-start | bytes 36868
  20.1 23.6 %copy-start.2 = (f32[2,12,128]{2,0,1:T(2,128)S(1)}, f32[2,12,128]{2,0,1:T(2,128)}, u32[]{:S(2)}) copy-start(f32[2,12,128]{2,0,1:T(2,128)} %param.10) | copy-start | bytes 36868
  20.1 23.6 %copy-start.3 = (f32[2,12,128]{2,0,1:T(2,128)S(1)}, f32[2,12,128]{2,0,1:T(2,128)}, u32[]{:S(2)}) copy-start(f32[2,12,128]{2,0,1:T(2,128)} %param.9) | copy-start | bytes 36868
  22.4 11.0 %all-to-all-start.1 = ((f32[32,9,1,128]{3,2,1,0:T(1,128)}), f32[32,9,1,128]{3,2,1,0:T(1,128)S(1)}, u32[]{:S(2)}, u32[]{:S(2)}) async-start(f32[32,9,1,128]{3,2,1,0:T(1,128)} %bitcast.10), calls=%async_computation.1 | async-start | bytes 294912 | tf_op jit(solution)/shard_map/all_to_all | solution.py:360
  25.0 3.3 %collective-permute-start.1 = (f32[18,128]{1,0:T(8,128)S(1)}, f32[18,128]{1,0:T(8,128)S(1)}, u32[]{:S(2)}, u32[]{:S(2)}) collective-permute-start(f32[18,128]{1,0:T(8,128)S(1)} %get-tuple-element.51), channel_id=1, source_target_pairs={{0,1},{1,2},{2,3},{3,0},{4,5},{5,6},{6,7},{7,4},{8,9},{9,10},{10,1... | collective-permute-start | bytes 27656 | tf_op jit(solution)/shard_map/ppermute | solution.py:467
  25.3 3.8 %collective-permute-start.2 = (f32[18,128]{1,0:T(8,128)S(1)}, f32[18,128]{1,0:T(8,128)S(1)}, u32[]{:S(2)}, u32[]{:S(2)}) collective-permute-start(f32[18,128]{1,0:T(8,128)S(1)} %get-tuple-element.52), channel_id=1, source_target_pairs={{0,2},{1,3},{2,0},{3,1},{4,6},{5,7},{6,4},{7,5},{8,10},{9,11},{10,... | collective-permute-start | bytes 27656 | tf_op jit(solution)/shard_map/ppermute | solution.py:467
  27.0 2.7 %collective-permute-start.3 = (f32[18,128]{1,0:T(8,128)S(1)}, f32[18,128]{1,0:T(8,128)S(1)}, u32[]{:S(2)}, u32[]{:S(2)}) collective-permute-start(f32[18,128]{1,0:T(8,128)S(1)} %get-tuple-element.53), channel_id=1, source_target_pairs={{0,3},{1,0},{2,1},{3,2},{4,7},{5,4},{6,5},{7,6},{8,11},{9,8},{10,9... | collective-permute-start | bytes 27656 | tf_op jit(solution)/shard_map/ppermute | solution.py:467

commit v2 on v1

--- a/solution.py
+++ b/solution.py
@@ -1,3 +1,4 @@
+import dataclasses
 import functools
 
 import jax
@@ -47,7 +48,7 @@
     lists[...] = jnp.zeros_like(lists)
     for s in range(slot_count):
         row, lane = divmod(s * owners, LANES)
-        moved = source[rows + s : rows + s + 1, :]
+        moved = source[rows + s]
         if lane:
             moved = pltpu.roll(moved, lane, 1)
         lists[row : row + 1, :] = lists[row : row + 1, :] + moved
@@ -55,7 +56,8 @@
     halves_of[...] = jnp.zeros_like(halves_of)
     for c in range(pieces):
         at = (c % 2) * size + (c // 2) * piece
-        halves_of[at : at + piece, :] = source[c * piece : (c + 1) * piece, :]
+        for line in range(piece):
+            halves_of[at + line : at + line + 1, :] = source[c * piece + line]
     for parity in range(2):
         at = parity * size + half_rows
         halves_of[at : at + extra, :] = lists[0:extra, :]
@@ -399,9 +401,9 @@
             pltpu.VMEM((-(-2 * size // 8) * 8, lanes), f32),
             pltpu.VMEM((-(-extra // 8) * 8, lanes), f32),
         ],
-        compiler_params=asked,
+        compiler_params=dataclasses.replace(asked, allow_input_fusion=(True,)),
         name="pack",
-    )(source.reshape(-1, lanes))
+    )(source)
     packed, rigid_nbr, node_refs = lax.optimization_barrier((packed, rigid_nbr, node_refs))
     gathered = exchange(packed, AXES)
 

time: 44.9 us -> 44.9 us (level)
  no operation moved by 1% of the time
where the time goes in v2:
time: 44.9 us; the launch traced here: 44.4 us
  starting transfers between devices  13.6 us (30%)
  waiting for transfers between devices  10.5 us (23%)
  blocking collectives  9.95 us (22%)
  Pallas kernels  6.52 us (15%)
  other arithmetic  2.41 us (5%)
  between operations  0.73 us (2%)
  local copies, waits for them, and re-layouts  0.7 us (2%)
    all_to_all x1, blocking collectives, exchange(): lax.all_to_all(blocks, axes, split_axis=0, concat_axis=0, tiled=True)  9.95 us
    all_to_all x2, starting transfers between devices, exchange(): lax.all_to_all(blocks, axes, split_axis=0, concat_axis=0, tiled=True)  9.88 us
    all_to_all x2, waiting for transfers between devices, exchange(): lax.all_to_all(blocks, axes, split_axis=0, concat_axis=0, tiled=True)  8.71 us
    ppermute x3, starting transfers between devices, on_device(): mine.append(lax.ppermute(pieces[distance], 'cams', turn))  3.3 us
    add x3, other arithmetic, joined_rows(): total = value if total is None else total + value  2.41 us
    pallas_call x1, Pallas kernels, on_device(): pl.pallas_call(functools.partial(data_kernel, sizes), out_shape=(array(de...  1.92 us
    ppermute x3, waiting for transfers between devices, on_device(): mine.append(lax.ppermute(pieces[distance], 'cams', turn))  1.4 us
    pallas_call x1, Pallas kernels, on_device(): pl.pallas_call(functools.partial(masks_kernel, params, node_refs.shape[0]...  1.15 us
  transfers between devices with their start and end apart: 6, of which 5 were waited for; matrix products, arithmetic and copies ran while one was open for 4% of the time, Pallas kernels for 6%

profile of v2, /device:TPU:0, one launch (start us, length us, event | category | flops | bytes accessed | tf_op | source)
XLA Modules:
  0.0 44.4 jit_solution(9426796748114247353)
XLA Ops:
  0.6 0.7 %convert_add_fusion.2.source = f32[32,1,128]{2,1,0:T(1,128)S(1)} fusion(s32[3,1,8]{2,1,0:T(1,128)} %bitcast.45, f32[24,1,128]{2,1,0:T(1,128)} %bitcast.37), kind=kLoop, calls=%fused_computation.2 | loop fusion | flops 8192 | bytes 28768 | tf_op jit(solution)/shard_map/add | solution.py:353
  1.4 0.8 %pack.1 = f32[416,128]{1,0:T(8,128)} custom-call(f32[32,1,128]{2,1,0:T(1,128)S(1)} %convert_add_fusion.2.source), custom_call_target="tpu_custom_call" | custom-call | tf_op jit(solution)/shard_map/pack/pallas_call | solution.py:393
  2.1 7.3 %all-to-all-start = ((f32[32,13,1,128]{3,2,1,0:T(1,128)}), f32[32,13,1,128]{3,2,1,0:T(1,128)S(1)}, u32[]{:S(2)}, u32[]{:S(2)}) async-start(f32[32,13,1,128]{3,2,1,0:T(1,128)} %bitcast.7), calls=%async_computation | async-start | bytes 425984 | tf_op jit(solution)/shard_map/all_to_all | solution.py:362
  9.5 0.8 %convert_add_fusion.1 = f32[48,2,128]{2,1,0:T(2,128)S(1)} fusion(s32[6,2,128]{2,1,0:T(2,128)} %bitcast.47, f32[12,2,128]{2,1,0:T(2,128)} %bitcast.40, f32[12,2,128]{2,1,0:T(2,128)} %bitcast.42, f32[12,2,128]{2,1,0:T(2,128)} %bitcast.38), kind=kLoop, calls=%fused_computation.1 | loop fusion | flops 49152 | bytes 92160 | tf_op jit(solution)/shard_map/add | solution.py:353
  10.2 0.0 copy-start.4
  10.2 0.7 %copy-done.4 = s32[1,8,3]{1,0,2:T(1,128)S(1)} copy-done((s32[1,8,3]{1,0,2:T(1,128)S(1)}, s32[1,8,3]{1,0,2:T(1,128)}, u32[]{:S(2)}) %copy-start.4) | copy-done | bytes 120
  10.9 0.8 %near.1 = (f32[8,128]{1,0:T(8,128)S(1)}, bf16[32,288]{1,0:T(8,128)(2,1)S(1)}, f32[18,128]{1,0:T(8,128)S(1)}, f32[18,128]{1,0:T(8,128)S(1)}, f32[18,128]{1,0:T(8,128)S(1)}, /*index=5*/f32[18,128]{1,0:T(8,128)S(1)}) custom-call(s32[3,1,8]{2,1,0:T(1,128)S(1)} %bitcast.46, f32[96,128]{1,0:T(8,128)S(1)} %bitcast.36), custom_call_target="tpu_custom_call" | custom-call | tf_op jit(solution)/shard_map/near/pallas_call | solution.py:415
  11.8 0.9 %convert_add_fusion.pixel_rows = f32[24,2048]{1,0:T(8,128)S(1)} fusion(s32[4,2048]{1,0:T(4,128)} %param.15, bf16[4,2048]{1,0:T(4,128)(2,1)} %param.16, bf16[12,2048]{1,0:T(8,128)(2,1)} %param.14), kind=kLoop, calls=%fused_computation | loop fusion | flops 245760 | bytes 294912 | tf_op jit(solution)/shard_map/add | solution.py:353
  12.7 1.1 %masks.1 = (f32[128,2048]{1,0:T(8,128)S(1)}, bf16[384,2048]{1,0:T(8,128)(2,1)S(1)}) custom-call(f32[24,2048]{1,0:T(8,128)S(1)} %convert_add_fusion.pixel_rows), custom_call_target="tpu_custom_call" | custom-call | tf_op jit(solution)/shard_map/masks/pallas_call | solution.py:425
  13.8 5.0 %all-to-all-done = f32[32,13,1,128]{3,2,1,0:T(1,128)S(1)} async-done(((f32[32,13,1,128]{3,2,1,0:T(1,128)}), f32[32,13,1,128]{3,2,1,0:T(1,128)S(1)}, u32[]{:S(2)}, u32[]{:S(2)}) %all-to-all-start) | async-done | bytes 213024 | tf_op jit(solution)/shard_map/all_to_all | solution.py:362
  18.8 0.3 table.1
  19.2 0.4 collective-permute-start
  19.6 0.5 %own_half.1.pulled_own = f32[128,2048]{1,0:T(8,128)S(1)} custom-call(f32[192,128]{1,0:T(8,128)S(1)} %get-tuple-element.37.table, bf16[384,2048]{1,0:T(8,128)(2,1)S(1)} %get-tuple-element.38.masked), custom_call_target="tpu_custom_call" | custom-call | tf_op jit(solution)/shard_map/own_half/pallas_call | solution.py:447
  20.0 0.0 copy-start
  20.0 0.0 copy-start.1
  20.1 0.0 copy-start.2
  20.1 0.0 copy-start.3
  20.1 0.4 collective-permute-done.table
  20.5 1.9 %data_products.1 = (f32[288,128]{1,0:T(8,128)}, f32[8,128]{1,0:T(8,128)S(1)}) custom-call(f32[128,2048]{1,0:T(8,128)S(1)} %own_half.1.pulled_own, f32[192,128]{1,0:T(8,128)S(1)} %collective-permute-done.table, f32[128,2048]{1,0:T(8,128)S(1)} %get-tuple-element.39.spread, bf16[384,2048]{1,0:T(8,128)(2,1)S(1)} %get-tuple-element.38.masked), custom_call_target="tpu_custom_call" | custom-call | tf_op jit(solution)/shard_map/data_products/pallas_call | solution.py:455
  22.4 2.6 %all-to-all-start.1 = ((f32[32,9,1,128]{3,2,1,0:T(1,128)}), f32[32,9,1,128]{3,2,1,0:T(1,128)S(1)}, u32[]{:S(2)}, u32[]{:S(2)}) async-start(f32[32,9,1,128]{3,2,1,0:T(1,128)} %bitcast.9), calls=%async_computation.1 | async-start | bytes 294912 | tf_op jit(solution)/shard_map/all_to_all | solution.py:362
  25.0 0.3 collective-permute-start.1
  25.3 1.7 %collective-permute-start.2 = (f32[18,128]{1,0:T(8,128)S(1)}, f32[18,128]{1,0:T(8,128)S(1)}, u32[]{:S(2)}, u32[]{:S(2)}) collective-permute-start(f32[18,128]{1,0:T(8,128)S(1)} %get-tuple-element.52), channel_id=1, source_target_pairs={{0,2},{1,3},{2,0},{3,1},{4,6},{5,7},{6,4},{7,5},{8,10},{9,11},{10,... | collective-permute-start | bytes 27656 | tf_op jit(solution)/shard_map/ppermute | solution.py:469
  27.0 1.3 %collective-permute-start.3 = (f32[18,128]{1,0:T(8,128)S(1)}, f32[18,128]{1,0:T(8,128)S(1)}, u32[]{:S(2)}, u32[]{:S(2)}) collective-permute-start(f32[18,128]{1,0:T(8,128)S(1)} %get-tuple-element.53), channel_id=1, source_target_pairs={{0,3},{1,0},{2,1},{3,2},{4,7},{5,4},{6,5},{7,6},{8,11},{9,8},{10,9... | collective-permute-start | bytes 27656 | tf_op jit(solution)/shard_map/ppermute | solution.py:469
  28.3 0.0 collective-permute-done.1.refs_1_
  28.3 0.8 %collective-permute-done.2.refs_2_ = f32[18,128]{1,0:T(8,128)S(1)} collective-permute-done((f32[18,128]{1,0:T(8,128)S(1)}, f32[18,128]{1,0:T(8,128)S(1)}, u32[]{:S(2)}, u32[]{:S(2)}) %collective-permute-start.2) | collective-permute-done | bytes 9248 | tf_op jit(solution)/shard_map/ppermute | solution.py:469
  29.1 0.6 %collective-permute-done.3.refs_3_ = f32[18,128]{1,0:T(8,128)S(1)} collective-permute-done((f32[18,128]{1,0:T(8,128)S(1)}, f32[18,128]{1,0:T(8,128)S(1)}, u32[]{:S(2)}, u32[]{:S(2)}) %collective-permute-start.3) | collective-permute-done | bytes 9248 | tf_op jit(solution)/shard_map/ppermute | solution.py:469
  29.7 3.7 %all-to-all-done.1 = f32[32,9,1,128]{3,2,1,0:T(1,128)S(1)} async-done(((f32[32,9,1,128]{3,2,1,0:T(1,128)}), f32[32,9,1,128]{3,2,1,0:T(1,128)S(1)}, u32[]{:S(2)}, u32[]{:S(2)}) %all-to-all-start.1) | async-done | bytes 147488 | tf_op jit(solution)/shard_map/all_to_all | solution.py:362
  33.4 0.3 image.1
  33.7 9.9 %all_to_all.15 = f32[32,7,1,128]{3,2,1,0:T(1,128)S(1)} all-to-all(f32[32,7,1,128]{3,2,1,0:T(1,128)S(1)} %bitcast.35), channel_id=1, replica_groups=mesh['nodes'=8,'cams'=4] {'nodes','cams'}, dimensions={0} | all-to-all | bytes 229376 | tf_op jit(solution)/shard_map/all_to_all | solution.py:362
  43.7 0.0 copy-done
  43.7 0.0 copy-done.1
  43.7 0.0 copy-done.2
  43.7 0.0 copy-done.3
  43.7 0.7 %update.1 = (f32[24,128]{1,0:T(8,128)}, f32[24,128]{1,0:T(8,128)}, f32[24,128]{1,0:T(8,128)}) custom-call(f32[224,128]{1,0:T(8,128)S(1)} %bitcast.34, f32[24,128]{1,0:T(8,128)S(1)} %bitcast.44, f32[24,128]{1,0:T(8,128)S(1)} %bitcast.43, f32[24,128]{1,0:T(8,128)S(1)} %bitcast.39, f32[24,128]{1,0:T(8,128)S(1)} %bitcast.41), custom_call_target="tpu_custom_call" | custom-call | tf_op jit(solution)/shard_map/update/pallas_call | solution.py:481
Async XLA Ops:
  2.1 16.7 %all-to-all-start = ((f32[32,13,1,128]{3,2,1,0:T(1,128)}), f32[32,13,1,128]{3,2,1,0:T(1,128)S(1)}, u32[]{:S(2)}, u32[]{:S(2)}) async-start(f32[32,13,1,128]{3,2,1,0:T(1,128)} %bitcast.7), calls=%async_computation | async-start | bytes 425984 | tf_op jit(solution)/shard_map/all_to_all | solution.py:362
  10.2 0.7 %copy-start.4 = (s32[1,8,3]{1,0,2:T(1,128)S(1)}, s32[1,8,3]{1,0,2:T(1,128)}, u32[]{:S(2)}) copy-start(s32[1,8,3]{1,0,2:T(1,128)} %param.13) | copy-start | bytes 292
  19.2 1.3 %collective-permute-start = (f32[192,128]{1,0:T(8,128)S(1)}, f32[192,128]{1,0:T(8,128)S(1)}, u32[]{:S(2)}, u32[]{:S(2)}) collective-permute-start(f32[192,128]{1,0:T(8,128)S(1)} %get-tuple-element.37.table), channel_id=1, source_target_pairs={{0,1},{1,0},{2,3},{3,2},{4,5},{5,4},{6,7},{7,6},{8,9},{9,8},{10,11... | collective-permute-start | bytes 294920 | tf_op jit(solution)/shard_map/ppermute | solution.py:446
  20.0 23.6 %copy-start = (f32[2,12,128]{2,0,1:T(2,128)S(1)}, f32[2,12,128]{2,0,1:T(2,128)}, u32[]{:S(2)}) copy-start(f32[2,12,128]{2,0,1:T(2,128)} %param.11) | copy-start | bytes 36868
  20.0 23.6 %copy-start.1 = (f32[2,12,128]{2,0,1:T(2,128)S(1)}, f32[2,12,128]{2,0,1:T(2,128)}, u32[]{:S(2)}) copy-start(f32[2,12,128]{2,0,1:T(2,128)} %param.12) | copy-start | bytes 36868
  20.1 23.6 %copy-start.2 = (f32[2,12,128]{2,0,1:T(2,128)S(1)}, f32[2,12,128]{2,0,1:T(2,128)}, u32[]{:S(2)}) copy-start(f32[2,12,128]{2,0,1:T(2,128)} %param.10) | copy-start | bytes 36868
  20.1 23.6 %copy-start.3 = (f32[2,12,128]{2,0,1:T(2,128)S(1)}, f32[2,12,128]{2,0,1:T(2,128)}, u32[]{:S(2)}) copy-start(f32[2,12,128]{2,0,1:T(2,128)} %param.9) | copy-start | bytes 36868
  22.4 11.0 %all-to-all-start.1 = ((f32[32,9,1,128]{3,2,1,0:T(1,128)}), f32[32,9,1,128]{3,2,1,0:T(1,128)S(1)}, u32[]{:S(2)}, u32[]{:S(2)}) async-start(f32[32,9,1,128]{3,2,1,0:T(1,128)} %bitcast.9), calls=%async_computation.1 | async-start | bytes 294912 | tf_op jit(solution)/shard_map/all_to_all | solution.py:362
  25.0 3.3 %collective-permute-start.1 = (f32[18,128]{1,0:T(8,128)S(1)}, f32[18,128]{1,0:T(8,128)S(1)}, u32[]{:S(2)}, u32[]{:S(2)}) collective-permute-start(f32[18,128]{1,0:T(8,128)S(1)} %get-tuple-element.51), channel_id=1, source_target_pairs={{0,1},{1,2},{2,3},{3,0},{4,5},{5,6},{6,7},{7,4},{8,9},{9,10},{10,1... | collective-permute-start | bytes 27656 | tf_op jit(solution)/shard_map/ppermute | solution.py:469
  25.3 3.8 %collective-permute-start.2 = (f32[18,128]{1,0:T(8,128)S(1)}, f32[18,128]{1,0:T(8,128)S(1)}, u32[]{:S(2)}, u32[]{:S(2)}) collective-permute-start(f32[18,128]{1,0:T(8,128)S(1)} %get-tuple-element.52), channel_id=1, source_target_pairs={{0,2},{1,3},{2,0},{3,1},{4,6},{5,7},{6,4},{7,5},{8,10},{9,11},{10,... | collective-permute-start | bytes 27656 | tf_op jit(solution)/shard_map/ppermute | solution.py:469
  27.0 2.7 %collective-permute-start.3 = (f32[18,128]{1,0:T(8,128)S(1)}, f32[18,128]{1,0:T(8,128)S(1)}, u32[]{:S(2)}, u32[]{:S(2)}) collective-permute-start(f32[18,128]{1,0:T(8,128)S(1)} %get-tuple-element.53), channel_id=1, source_target_pairs={{0,3},{1,0},{2,1},{3,2},{4,7},{5,4},{6,5},{7,6},{8,11},{9,8},{10,9... | collective-permute-start | bytes 27656 | tf_op jit(solution)/shard_map/ppermute | solution.py:469

commit v3 on v1

--- a/solution.py
+++ b/solution.py
@@ -113,7 +113,7 @@
 
     column = lax.broadcasted_iota(jnp.int32, (1, choose.shape[1]), 1)
     row = column % back_rows
-    slot = column // (back_rows * cams) * slot_count + row // part
+    slot = column // (back_rows * (cams // 2)) * slot_count + row // part
     listed = jnp.zeros_like(column)
     for owner in range(owners):
         for s in range(slot_count):
@@ -232,7 +232,7 @@
         pulled_out[:, cols] = pull(turned_table, masked, parity, cols)
 
 
-def data_kernel(sizes, pulled_own, table, spread, masked, out, squares_out, products):
+def data_kernel(sizes, pulled_own, table, spread, masked, keep, pass_on, squares_out, products, out):
     owners, cams, slot_count, held, params, part, half_pieces, extra, back_rows, step = sizes
     side = masked.shape[0] // 2
     parity = 1 - lax.rem(lax.axis_index("cams"), 2)
@@ -257,9 +257,11 @@
 
     squares_out[0:1, :] = squares
 
+    count = keep.shape[0]
+
     def give(owner):
         for c in range(cams):
-            base = (owner * cams + c) * back_rows
+            base = (c % 2) * count + (owner * (cams // 2) + c // 2) * back_rows
             for s in range(slot_count):
                 if c * part < params:
                     at = (c % 2) * side + (owner * slot_count + s) * HALF + (c // 2) * part
@@ -269,6 +271,12 @@
                 out[pl.ds(base + s * part, part), :] = value
 
     loop(owners, give)
+    keep[...] = out[pl.ds(pl.multiple_of((1 - parity) * count, 8), count), :]
+    pass_on[...] = out[pl.ds(pl.multiple_of(parity * count, 8), count), :]
+
+
+def sum_kernel(kept, passed, out):
+    out[...] = kept[...] + passed[...]
 
 
 def image_kernel(sizes, choose, received, frames, near_sums, frame_sums, squares, *refs):
@@ -412,7 +420,7 @@
     image_rows = -(-cams * piece // 16) * 16
     sums, choose, *pieces = pl.pallas_call(
         functools.partial(near_kernel, sizes, rows, rigid_nbr.shape[1]),
-        out_shape=(array(8), jax.ShapeDtypeStruct((image_rows, devices * back_rows), bf16))
+        out_shape=(array(8), jax.ShapeDtypeStruct((image_rows, devices // 2 * back_rows), bf16))
         + (array(3 * piece),) * cams,
         in_specs=[SMEM, VMEM],
         out_specs=(VMEM,) * (2 + cams),
@@ -450,17 +458,31 @@
         compiler_params=asked,
         name="own_half",
     )(table, masked)
-    products, squares = pl.pallas_call(
+    count = devices // 2 * back_rows
+    kept, passed, squares = pl.pallas_call(
         functools.partial(data_kernel, sizes),
-        out_shape=(array(devices * back_rows), array(8)),
+        out_shape=(array(count), array(count), array(8)),
         in_specs=[VMEM] * 4,
-        out_specs=(VMEM,) * 2,
-        scratch_shapes=[pltpu.VMEM((2 * side, lanes), f32)],
+        out_specs=(VMEM,) * 3,
+        scratch_shapes=[pltpu.VMEM((2 * side, lanes), f32), pltpu.VMEM((2 * count, lanes), f32)],
         compiler_params=asked,
         name="data_products",
     )(pulled, other, spread, masked)
+    passed = lax.ppermute(passed, "cams", [(c, c ^ 1) for c in range(cams)])
+    products = pl.pallas_call(
+        sum_kernel,
+        out_shape=array(count),
+        in_specs=[VMEM] * 2,
+        out_specs=VMEM,
+        compiler_params=asked,
+        name="pair_sum",
+    )(kept, passed)
     products, *pieces = lax.optimization_barrier((products, *pieces))
-    received = exchange(products, AXES)
+    alike = [[d for d in range(devices) if d % cams % 2 == parity] for parity in range(2)]
+    received = lax.all_to_all(
+        products.reshape(devices // 2, back_rows, 1, lanes),
+        AXES, split_axis=0, concat_axis=0, axis_index_groups=alike, tiled=True,
+    ).reshape(count, lanes)
     mine = [pieces[0]]
     for distance in range(1, cams):
         turn = [(c, (c + distance) % cams) for c in range(cams)]

time: 44.9 us -> 47.3 us (1.053)
  starting transfers between devices: 13.6 us -> 15.1 us
  blocking collectives: 9.95 us -> 10.7 us
    all_to_all x2 -> x1, waiting for transfers between devices: 8.71 us -> 5.02 us  [exchange(): lax.all_to_all(blocks, axes, split_axis=0, concat_axis=0, tiled=True)]
    all_to_all x0 -> x1, starting transfers between devices: none -> 3.59 us  [on_device(): lax.all_to_all(products.reshape(devices // 2, back_rows, 1, lanes), AXES,...]
    all_to_all x0 -> x1, waiting for transfers between devices: none -> 2.77 us  [on_device(): lax.all_to_all(products.reshape(devices // 2, back_rows, 1, lanes), AXES,...]
    all_to_all x2 -> x1, starting transfers between devices: 9.88 us -> 7.3 us  [exchange(): lax.all_to_all(blocks, axes, split_axis=0, concat_axis=0, tiled=True)]
    ppermute x0 -> x1, waiting for transfers between devices: none -> 0.91 us  [on_device(): passed = lax.ppermute(passed, 'cams', [(c, c ^ 1) for c in range(cams)])]
    all_to_all x1, blocking collectives: 9.95 us -> 10.7 us  [exchange(): lax.all_to_all(blocks, axes, split_axis=0, concat_axis=0, tiled=True)]
    pallas_call x1 -> x2, Pallas kernels: 1.92 us -> 1.92 us  [the longest x1 1.27 us: on_device(): pl.pallas_call(functools.partial(data_kernel, sizes), out_shape=(array(co...]
  transfers between devices with their start and end apart: 6 -> 7, of which waited for: 5 -> 6; matrix products, arithmetic and copies ran while one was open for 4% -> 4% of each run, Pallas kernels for 6% -> 5%
where the time goes in v3:
time: 47.3 us; the launch traced here: 46.7 us
  starting transfers between devices  15.1 us (32%)
  blocking collectives  10.7 us (23%)
  waiting for transfers between devices  10.5 us (22%)
  Pallas kernels  6.5 us (14%)
  other arithmetic  2.41 us (5%)
  between operations  0.73 us (2%)
  local copies, waits for them, and re-layouts  0.7 us (1%)
    all_to_all x1, blocking collectives, exchange(): lax.all_to_all(blocks, axes, split_axis=0, concat_axis=0, tiled=True)  10.7 us
    all_to_all x1, starting transfers between devices, exchange(): lax.all_to_all(blocks, axes, split_axis=0, concat_axis=0, tiled=True)  7.3 us
    all_to_all x1, waiting for transfers between devices, exchange(): lax.all_to_all(blocks, axes, split_axis=0, concat_axis=0, tiled=True)  5.02 us
    all_to_all x1, starting transfers between devices, on_device(): lax.all_to_all(products.reshape(devices // 2, back_rows, 1, lanes), AXES,...  3.59 us
    ppermute x3, starting transfers between devices, on_device(): mine.append(lax.ppermute(pieces[distance], 'cams', turn))  3.39 us
    all_to_all x1, waiting for transfers between devices, on_device(): lax.all_to_all(products.reshape(devices // 2, back_rows, 1, lanes), AXES,...  2.77 us
    add x3, other arithmetic, joined_rows(): total = value if total is None else total + value  2.41 us
    ppermute x3, waiting for transfers between devices, on_device(): mine.append(lax.ppermute(pieces[distance], 'cams', turn))  1.4 us
  transfers between devices with their start and end apart: 7, of which 6 were waited for; matrix products, arithmetic and copies ran while one was open for 4% of the time, Pallas kernels for 5%

profile of v3, /device:TPU:0, one launch (start us, length us, event | category | flops | bytes accessed | tf_op | source)
XLA Modules:
  0.0 46.7 jit_solution(14206055643584042521)
XLA Ops:
  0.6 0.7 %convert_add_fusion.2 = f32[32,1,128]{2,1,0:T(1,128)S(1)} fusion(s32[3,1,8]{2,1,0:T(1,128)} %bitcast.47, f32[24,1,128]{2,1,0:T(1,128)} %bitcast.38), kind=kLoop, calls=%fused_computation.2 | loop fusion | flops 8192 | bytes 28768 | tf_op jit(solution)/shard_map/add | solution.py:359
  1.4 0.8 %pack.1 = f32[416,128]{1,0:T(8,128)} custom-call(f32[32,128]{1,0:T(8,128)S(1)} %bitcast.41), custom_call_target="tpu_custom_call" | custom-call | tf_op jit(solution)/shard_map/pack/pallas_call | solution.py:399
  2.1 7.3 %all-to-all-start = ((f32[32,13,1,128]{3,2,1,0:T(1,128)}), f32[32,13,1,128]{3,2,1,0:T(1,128)S(1)}, u32[]{:S(2)}, u32[]{:S(2)}) async-start(f32[32,13,1,128]{3,2,1,0:T(1,128)} %bitcast.8), calls=%async_computation | async-start | bytes 425984 | tf_op jit(solution)/shard_map/all_to_all | solution.py:368
  9.5 0.8 %convert_add_fusion.1 = f32[48,2,128]{2,1,0:T(2,128)S(1)} fusion(s32[6,2,128]{2,1,0:T(2,128)} %bitcast.49, f32[12,2,128]{2,1,0:T(2,128)} %bitcast.42, f32[12,2,128]{2,1,0:T(2,128)} %bitcast.44, f32[12,2,128]{2,1,0:T(2,128)} %bitcast.39), kind=kLoop, calls=%fused_computation.1 | loop fusion | flops 49152 | bytes 92160 | tf_op jit(solution)/shard_map/add | solution.py:359
  10.2 0.0 copy-start.4
  10.2 0.7 %copy-done.4 = s32[1,8,3]{1,0,2:T(1,128)S(1)} copy-done((s32[1,8,3]{1,0,2:T(1,128)S(1)}, s32[1,8,3]{1,0,2:T(1,128)}, u32[]{:S(2)}) %copy-start.4) | copy-done | bytes 120
  10.9 0.8 %near.1 = (f32[8,128]{1,0:T(8,128)S(1)}, bf16[32,144]{1,0:T(8,128)(2,1)S(1)}, f32[18,128]{1,0:T(8,128)S(1)}, f32[18,128]{1,0:T(8,128)S(1)}, f32[18,128]{1,0:T(8,128)S(1)}, /*index=5*/f32[18,128]{1,0:T(8,128)S(1)}) custom-call(s32[3,1,8]{2,1,0:T(1,128)S(1)} %bitcast.48, f32[96,128]{1,0:T(8,128)S(1)} %bitcast.37), custom_call_target="tpu_custom_call" | custom-call | tf_op jit(solution)/shard_map/near/pallas_call | solution.py:421
  11.7 0.9 %convert_add_fusion.pixel_rows = f32[24,2048]{1,0:T(8,128)S(1)} fusion(s32[4,2048]{1,0:T(4,128)} %param.15, bf16[4,2048]{1,0:T(4,128)(2,1)} %param.16, bf16[12,2048]{1,0:T(8,128)(2,1)} %param.14), kind=kLoop, calls=%fused_computation | loop fusion | flops 245760 | bytes 294912 | tf_op jit(solution)/shard_map/add | solution.py:359
  12.7 1.1 %masks.1 = (f32[128,2048]{1,0:T(8,128)S(1)}, bf16[384,2048]{1,0:T(8,128)(2,1)S(1)}) custom-call(f32[24,2048]{1,0:T(8,128)S(1)} %convert_add_fusion.pixel_rows), custom_call_target="tpu_custom_call" | custom-call | tf_op jit(solution)/shard_map/masks/pallas_call | solution.py:431
  13.8 5.0 %all-to-all-done = f32[32,13,1,128]{3,2,1,0:T(1,128)S(1)} async-done(((f32[32,13,1,128]{3,2,1,0:T(1,128)}), f32[32,13,1,128]{3,2,1,0:T(1,128)S(1)}, u32[]{:S(2)}, u32[]{:S(2)}) %all-to-all-start) | async-done | bytes 213024 | tf_op jit(solution)/shard_map/all_to_all | solution.py:368
  18.8 0.3 table.1
  19.2 0.4 collective-permute-start
  19.6 0.5 own_half.1.pulled_own
  20.0 0.0 copy-start
  20.0 0.0 copy-start.1
  20.1 0.0 copy-start.2
  20.1 0.0 copy-start.3
  20.1 0.4 collective-permute-done.table
  20.5 1.3 %data_products.1 = (f32[144,128]{1,0:T(8,128)S(1)}, f32[144,128]{1,0:T(8,128)S(1)}, f32[8,128]{1,0:T(8,128)S(1)}) custom-call(f32[128,2048]{1,0:T(8,128)S(1)} %own_half.1.pulled_own, f32[192,128]{1,0:T(8,128)S(1)} %collective-permute-done.table, f32[128,2048]{1,0:T(8,128)S(1)} %get-tuple-element.40.spread, bf16[384,2048]{1,0:T(8,128)(2,1)S(1)} %get-tuple-element.39.masked), custom_call_target="tpu_custom_call" | custom-call | tf_op jit(solution)/shard_map/data_products/pallas_call | solution.py:462
  21.8 0.4 collective-permute-start.1
  22.2 0.9 %collective-permute-done.1.passed = f32[144,128]{1,0:T(8,128)S(1)} collective-permute-done((f32[144,128]{1,0:T(8,128)S(1)}, f32[144,128]{1,0:T(8,128)S(1)}, u32[]{:S(2)}, u32[]{:S(2)}) %collective-permute-start.1) | collective-permute-done | bytes 73760 | tf_op jit(solution)/shard_map/ppermute | solution.py:471
  23.1 0.7 %pair_sum.1 = f32[144,128]{1,0:T(8,128)} custom-call(f32[144,128]{1,0:T(8,128)S(1)} %get-tuple-element.41.kept, f32[144,128]{1,0:T(8,128)S(1)} %collective-permute-done.1.passed), custom_call_target="tpu_custom_call" | custom-call | tf_op jit(solution)/shard_map/pair_sum/pallas_call | solution.py:472
  23.8 3.6 %all-to-all-start.1 = ((f32[16,9,1,128]{3,2,1,0:T(1,128)}), f32[16,9,1,128]{3,2,1,0:T(1,128)S(1)}, u32[]{:S(2)}, u32[]{:S(2)}) async-start(f32[16,9,1,128]{3,2,1,0:T(1,128)} %bitcast.10), calls=%async_computation.1 | async-start | bytes 147456 | tf_op jit(solution)/shard_map/all_to_all | solution.py:482
  27.3 0.3 collective-permute-start.2
  27.7 1.7 %collective-permute-start.3 = (f32[18,128]{1,0:T(8,128)S(1)}, f32[18,128]{1,0:T(8,128)S(1)}, u32[]{:S(2)}, u32[]{:S(2)}) collective-permute-start(f32[18,128]{1,0:T(8,128)S(1)} %get-tuple-element.54), channel_id=1, source_target_pairs={{0,2},{1,3},{2,0},{3,1},{4,6},{5,7},{6,4},{7,5},{8,10},{9,11},{10,... | collective-permute-start | bytes 27656 | tf_op jit(solution)/shard_map/ppermute | solution.py:489
  29.4 1.4 %collective-permute-start.4 = (f32[18,128]{1,0:T(8,128)S(1)}, f32[18,128]{1,0:T(8,128)S(1)}, u32[]{:S(2)}, u32[]{:S(2)}) collective-permute-start(f32[18,128]{1,0:T(8,128)S(1)} %get-tuple-element.55), channel_id=1, source_target_pairs={{0,3},{1,0},{2,1},{3,2},{4,7},{5,4},{6,5},{7,6},{8,11},{9,8},{10,9... | collective-permute-start | bytes 27656 | tf_op jit(solution)/shard_map/ppermute | solution.py:489
  30.7 0.0 collective-permute-done.2.refs_1_
  30.7 0.7 %collective-permute-done.3.refs_2_ = f32[18,128]{1,0:T(8,128)S(1)} collective-permute-done((f32[18,128]{1,0:T(8,128)S(1)}, f32[18,128]{1,0:T(8,128)S(1)}, u32[]{:S(2)}, u32[]{:S(2)}) %collective-permute-start.3) | collective-permute-done | bytes 9248 | tf_op jit(solution)/shard_map/ppermute | solution.py:489
  31.4 0.7 %collective-permute-done.4.refs_3_ = f32[18,128]{1,0:T(8,128)S(1)} collective-permute-done((f32[18,128]{1,0:T(8,128)S(1)}, f32[18,128]{1,0:T(8,128)S(1)}, u32[]{:S(2)}, u32[]{:S(2)}) %collective-permute-start.4) | collective-permute-done | bytes 9248 | tf_op jit(solution)/shard_map/ppermute | solution.py:489
  32.1 2.8 %all-to-all-done.1 = f32[16,9,1,128]{3,2,1,0:T(1,128)S(1)} async-done(((f32[16,9,1,128]{3,2,1,0:T(1,128)}), f32[16,9,1,128]{3,2,1,0:T(1,128)S(1)}, u32[]{:S(2)}, u32[]{:S(2)}) %all-to-all-start.1) | async-done | bytes 73760 | tf_op jit(solution)/shard_map/all_to_all | solution.py:482
  34.9 0.3 image.1
  35.2 10.7 %all_to_all.15 = f32[32,7,1,128]{3,2,1,0:T(1,128)S(1)} all-to-all(f32[32,7,1,128]{3,2,1,0:T(1,128)S(1)} %bitcast.35), channel_id=1, replica_groups=mesh['nodes'=8,'cams'=4] {'nodes','cams'}, dimensions={0} | all-to-all | bytes 229376 | tf_op jit(solution)/shard_map/all_to_all | solution.py:368
  46.0 0.0 copy-done
  46.0 0.0 copy-done.1
  46.0 0.0 copy-done.2
  46.0 0.0 copy-done.3
  46.0 0.7 %update.1 = (f32[24,128]{1,0:T(8,128)}, f32[24,128]{1,0:T(8,128)}, f32[24,128]{1,0:T(8,128)}) custom-call(f32[224,128]{1,0:T(8,128)S(1)} %bitcast.34, f32[24,128]{1,0:T(8,128)S(1)} %bitcast.46, f32[24,128]{1,0:T(8,128)S(1)} %bitcast.45, f32[24,128]{1,0:T(8,128)S(1)} %bitcast.40, f32[24,128]{1,0:T(8,128)S(1)} %bitcast.43), custom_call_target="tpu_custom_call" | custom-call | tf_op jit(solution)/shard_map/update/pallas_call | solution.py:501
Async XLA Ops:
  2.1 16.7 %all-to-all-start = ((f32[32,13,1,128]{3,2,1,0:T(1,128)}), f32[32,13,1,128]{3,2,1,0:T(1,128)S(1)}, u32[]{:S(2)}, u32[]{:S(2)}) async-start(f32[32,13,1,128]{3,2,1,0:T(1,128)} %bitcast.8), calls=%async_computation | async-start | bytes 425984 | tf_op jit(solution)/shard_map/all_to_all | solution.py:368
  10.2 0.7 %copy-start.4 = (s32[1,8,3]{1,0,2:T(1,128)S(1)}, s32[1,8,3]{1,0,2:T(1,128)}, u32[]{:S(2)}) copy-start(s32[1,8,3]{1,0,2:T(1,128)} %param.13) | copy-start | bytes 292
  19.2 1.3 %collective-permute-start = (f32[192,128]{1,0:T(8,128)S(1)}, f32[192,128]{1,0:T(8,128)S(1)}, u32[]{:S(2)}, u32[]{:S(2)}) collective-permute-start(f32[192,128]{1,0:T(8,128)S(1)} %get-tuple-element.38.table), channel_id=1, source_target_pairs={{0,1},{1,0},{2,3},{3,2},{4,5},{5,4},{6,7},{7,6},{8,9},{9,8},{10,11... | collective-permute-start | bytes 294920 | tf_op jit(solution)/shard_map/ppermute | solution.py:452
  20.0 25.9 %copy-start = (f32[2,12,128]{2,0,1:T(2,128)S(1)}, f32[2,12,128]{2,0,1:T(2,128)}, u32[]{:S(2)}) copy-start(f32[2,12,128]{2,0,1:T(2,128)} %param.11) | copy-start | bytes 36868
  20.0 25.9 %copy-start.1 = (f32[2,12,128]{2,0,1:T(2,128)S(1)}, f32[2,12,128]{2,0,1:T(2,128)}, u32[]{:S(2)}) copy-start(f32[2,12,128]{2,0,1:T(2,128)} %param.12) | copy-start | bytes 36868
  20.1 25.9 %copy-start.2 = (f32[2,12,128]{2,0,1:T(2,128)S(1)}, f32[2,12,128]{2,0,1:T(2,128)}, u32[]{:S(2)}) copy-start(f32[2,12,128]{2,0,1:T(2,128)} %param.10) | copy-start | bytes 36868
  20.1 25.9 %copy-start.3 = (f32[2,12,128]{2,0,1:T(2,128)S(1)}, f32[2,12,128]{2,0,1:T(2,128)}, u32[]{:S(2)}) copy-start(f32[2,12,128]{2,0,1:T(2,128)} %param.9) | copy-start | bytes 36868
  21.8 1.3 %collective-permute-start.1 = (f32[144,128]{1,0:T(8,128)S(1)}, f32[144,128]{1,0:T(8,128)S(1)}, u32[]{:S(2)}, u32[]{:S(2)}) collective-permute-start(f32[144,128]{1,0:T(8,128)S(1)} %get-tuple-element.42), channel_id=1, source_target_pairs={{0,1},{1,0},{2,3},{3,2},{4,5},{5,4},{6,7},{7,6},{8,9},{9,8},{10,11... | collective-permute-start | bytes 221192 | tf_op jit(solution)/shard_map/ppermute | solution.py:471
  23.8 11.2 %all-to-all-start.1 = ((f32[16,9,1,128]{3,2,1,0:T(1,128)}), f32[16,9,1,128]{3,2,1,0:T(1,128)S(1)}, u32[]{:S(2)}, u32[]{:S(2)}) async-start(f32[16,9,1,128]{3,2,1,0:T(1,128)} %bitcast.10), calls=%async_computation.1 | async-start | bytes 147456 | tf_op jit(solution)/shard_map/all_to_all | solution.py:482
  27.3 3.4 %collective-permute-start.2 = (f32[18,128]{1,0:T(8,128)S(1)}, f32[18,128]{1,0:T(8,128)S(1)}, u32[]{:S(2)}, u32[]{:S(2)}) collective-permute-start(f32[18,128]{1,0:T(8,128)S(1)} %get-tuple-element.53), channel_id=1, source_target_pairs={{0,1},{1,2},{2,3},{3,0},{4,5},{5,6},{6,7},{7,4},{8,9},{9,10},{10,1... | collective-permute-start | bytes 27656 | tf_op jit(solution)/shard_map/ppermute | solution.py:489
  27.7 3.7 %collective-permute-start.3 = (f32[18,128]{1,0:T(8,128)S(1)}, f32[18,128]{1,0:T(8,128)S(1)}, u32[]{:S(2)}, u32[]{:S(2)}) collective-permute-start(f32[18,128]{1,0:T(8,128)S(1)} %get-tuple-element.54), channel_id=1, source_target_pairs={{0,2},{1,3},{2,0},{3,1},{4,6},{5,7},{6,4},{7,5},{8,10},{9,11},{10,... | collective-permute-start | bytes 27656 | tf_op jit(solution)/shard_map/ppermute | solution.py:489
  29.4 2.8 %collective-permute-start.4 = (f32[18,128]{1,0:T(8,128)S(1)}, f32[18,128]{1,0:T(8,128)S(1)}, u32[]{:S(2)}, u32[]{:S(2)}) collective-permute-start(f32[18,128]{1,0:T(8,128)S(1)} %get-tuple-element.55), channel_id=1, source_target_pairs={{0,3},{1,0},{2,1},{3,2},{4,7},{5,4},{6,5},{7,6},{8,11},{9,8},{10,9... | collective-permute-start | bytes 27656 | tf_op jit(solution)/shard_map/ppermute | solution.py:489

commit v4 on v1

--- a/solution.py
+++ b/solution.py
@@ -226,7 +226,7 @@
 def own_kernel(table, masked, pulled_out):
     parity = lax.rem(lax.axis_index("cams"), 2)
     turned_table = turned_halves(table)
-    chunk = 512
+    chunk = min(1024, masked.shape[1])
     for at in range(0, masked.shape[1], chunk):
         cols = slice(at, at + chunk)
         pulled_out[:, cols] = pull(turned_table, masked, parity, cols)
@@ -238,7 +238,7 @@
     parity = 1 - lax.rem(lax.axis_index("cams"), 2)
     turned_table = turned_halves(table)
     squares = jnp.zeros((1, LANES), f32)
-    chunk = 512
+    chunk = min(1024, masked.shape[1])
     for at in range(0, spread.shape[1], chunk):
         cols = slice(at, at + chunk)
         weights = spread[:, cols]

time: 44.9 us -> 44.7 us (level)
  no operation moved by 1% of the time
where the time goes in v4:
time: 44.7 us; the launch traced here: 44.2 us
  starting transfers between devices  13.6 us (30%)
  waiting for transfers between devices  10.5 us (23%)
  blocking collectives  9.95 us (22%)
  Pallas kernels  6.3 us (14%)
  other arithmetic  2.41 us (5%)
  between operations  0.73 us (2%)
  local copies, waits for them, and re-layouts  0.7 us (2%)
    all_to_all x1, blocking collectives, exchange(): lax.all_to_all(blocks, axes, split_axis=0, concat_axis=0, tiled=True)  9.95 us
    all_to_all x2, starting transfers between devices, exchange(): lax.all_to_all(blocks, axes, split_axis=0, concat_axis=0, tiled=True)  9.88 us
    all_to_all x2, waiting for transfers between devices, exchange(): lax.all_to_all(blocks, axes, split_axis=0, concat_axis=0, tiled=True)  8.71 us
    ppermute x3, starting transfers between devices, on_device(): mine.append(lax.ppermute(pieces[distance], 'cams', turn))  3.3 us
    add x3, other arithmetic, joined_rows(): total = value if total is None else total + value  2.41 us
    pallas_call x1, Pallas kernels, on_device(): pl.pallas_call(functools.partial(data_kernel, sizes), out_shape=(array(de...  1.7 us
    ppermute x3, waiting for transfers between devices, on_device(): mine.append(lax.ppermute(pieces[distance], 'cams', turn))  1.4 us
    pallas_call x1, Pallas kernels, on_device(): pl.pallas_call(functools.partial(masks_kernel, params, node_refs.shape[0]...  1.15 us
  transfers between devices with their start and end apart: 6, of which 5 were waited for; matrix products, arithmetic and copies ran while one was open for 4% of the time, Pallas kernels for 6%

profile of v4, /device:TPU:0, one launch (start us, length us, event | category | flops | bytes accessed | tf_op | source)
XLA Modules:
  0.0 44.2 jit_solution(3376112939688942360)
XLA Ops:
  0.6 0.7 %convert_add_fusion.2 = f32[32,1,128]{2,1,0:T(1,128)S(1)} fusion(s32[3,1,8]{2,1,0:T(1,128)} %bitcast.47, f32[24,1,128]{2,1,0:T(1,128)} %bitcast.38), kind=kLoop, calls=%fused_computation.2 | loop fusion | flops 8192 | bytes 28768 | tf_op jit(solution)/shard_map/add | solution.py:351
  1.4 0.8 %pack.1 = f32[416,128]{1,0:T(8,128)} custom-call(f32[32,128]{1,0:T(8,128)S(1)} %bitcast.41), custom_call_target="tpu_custom_call" | custom-call | tf_op jit(solution)/shard_map/pack/pallas_call | solution.py:391
  2.1 7.3 %all-to-all-start = ((f32[32,13,1,128]{3,2,1,0:T(1,128)}), f32[32,13,1,128]{3,2,1,0:T(1,128)S(1)}, u32[]{:S(2)}, u32[]{:S(2)}) async-start(f32[32,13,1,128]{3,2,1,0:T(1,128)} %bitcast.8), calls=%async_computation | async-start | bytes 425984 | tf_op jit(solution)/shard_map/all_to_all | solution.py:360
  9.5 0.8 %convert_add_fusion.1 = f32[48,2,128]{2,1,0:T(2,128)S(1)} fusion(s32[6,2,128]{2,1,0:T(2,128)} %bitcast.49, f32[12,2,128]{2,1,0:T(2,128)} %bitcast.42, f32[12,2,128]{2,1,0:T(2,128)} %bitcast.44, f32[12,2,128]{2,1,0:T(2,128)} %bitcast.39), kind=kLoop, calls=%fused_computation.1 | loop fusion | flops 49152 | bytes 92160 | tf_op jit(solution)/shard_map/add | solution.py:351
  10.2 0.0 copy-start.4
  10.2 0.7 %copy-done.4 = s32[1,8,3]{1,0,2:T(1,128)S(1)} copy-done((s32[1,8,3]{1,0,2:T(1,128)S(1)}, s32[1,8,3]{1,0,2:T(1,128)}, u32[]{:S(2)}) %copy-start.4) | copy-done | bytes 120
  10.9 0.8 %near.1 = (f32[8,128]{1,0:T(8,128)S(1)}, bf16[32,288]{1,0:T(8,128)(2,1)S(1)}, f32[18,128]{1,0:T(8,128)S(1)}, f32[18,128]{1,0:T(8,128)S(1)}, f32[18,128]{1,0:T(8,128)S(1)}, /*index=5*/f32[18,128]{1,0:T(8,128)S(1)}) custom-call(s32[3,1,8]{2,1,0:T(1,128)S(1)} %bitcast.48, f32[96,128]{1,0:T(8,128)S(1)} %bitcast.37), custom_call_target="tpu_custom_call" | custom-call | tf_op jit(solution)/shard_map/near/pallas_call | solution.py:413
  11.8 0.9 %convert_add_fusion.pixel_rows = f32[24,2048]{1,0:T(8,128)S(1)} fusion(s32[4,2048]{1,0:T(4,128)} %param.15, bf16[4,2048]{1,0:T(4,128)(2,1)} %param.16, bf16[12,2048]{1,0:T(8,128)(2,1)} %param.14), kind=kLoop, calls=%fused_computation | loop fusion | flops 245760 | bytes 294912 | tf_op jit(solution)/shard_map/add | solution.py:351
  12.7 1.1 %masks.1 = (f32[128,2048]{1,0:T(8,128)S(1)}, bf16[384,2048]{1,0:T(8,128)(2,1)S(1)}) custom-call(f32[24,2048]{1,0:T(8,128)S(1)} %convert_add_fusion.pixel_rows), custom_call_target="tpu_custom_call" | custom-call | tf_op jit(solution)/shard_map/masks/pallas_call | solution.py:423
  13.8 5.0 %all-to-all-done = f32[32,13,1,128]{3,2,1,0:T(1,128)S(1)} async-done(((f32[32,13,1,128]{3,2,1,0:T(1,128)}), f32[32,13,1,128]{3,2,1,0:T(1,128)S(1)}, u32[]{:S(2)}, u32[]{:S(2)}) %all-to-all-start) | async-done | bytes 213024 | tf_op jit(solution)/shard_map/all_to_all | solution.py:360
  18.8 0.3 table.1
  19.2 0.4 collective-permute-start
  19.6 0.5 %own_half.1.pulled_own = f32[128,2048]{1,0:T(8,128)S(1)} custom-call(f32[192,128]{1,0:T(8,128)S(1)} %get-tuple-element.37.table, bf16[384,2048]{1,0:T(8,128)(2,1)S(1)} %get-tuple-element.38.masked), custom_call_target="tpu_custom_call" | custom-call | tf_op jit(solution)/shard_map/own_half/pallas_call | solution.py:445
  20.0 0.0 copy-start
  20.0 0.0 copy-start.1
  20.1 0.0 copy-start.2
  20.1 0.0 copy-start.3
  20.1 0.4 collective-permute-done.table
  20.5 1.7 %data_products.1 = (f32[288,128]{1,0:T(8,128)}, f32[8,128]{1,0:T(8,128)S(1)}) custom-call(f32[128,2048]{1,0:T(8,128)S(1)} %own_half.1.pulled_own, f32[192,128]{1,0:T(8,128)S(1)} %collective-permute-done.table, f32[128,2048]{1,0:T(8,128)S(1)} %get-tuple-element.39.spread, bf16[384,2048]{1,0:T(8,128)(2,1)S(1)} %get-tuple-element.38.masked), custom_call_target="tpu_custom_call" | custom-call | tf_op jit(solution)/shard_map/data_products/pallas_call | solution.py:453
  22.2 2.6 %all-to-all-start.1 = ((f32[32,9,1,128]{3,2,1,0:T(1,128)}), f32[32,9,1,128]{3,2,1,0:T(1,128)S(1)}, u32[]{:S(2)}, u32[]{:S(2)}) async-start(f32[32,9,1,128]{3,2,1,0:T(1,128)} %bitcast.10), calls=%async_computation.1 | async-start | bytes 294912 | tf_op jit(solution)/shard_map/all_to_all | solution.py:360
  24.8 0.3 collective-permute-start.1
  25.1 1.7 %collective-permute-start.2 = (f32[18,128]{1,0:T(8,128)S(1)}, f32[18,128]{1,0:T(8,128)S(1)}, u32[]{:S(2)}, u32[]{:S(2)}) collective-permute-start(f32[18,128]{1,0:T(8,128)S(1)} %get-tuple-element.52), channel_id=1, source_target_pairs={{0,2},{1,3},{2,0},{3,1},{4,6},{5,7},{6,4},{7,5},{8,10},{9,11},{10,... | collective-permute-start | bytes 27656 | tf_op jit(solution)/shard_map/ppermute | solution.py:467
  26.8 1.3 %collective-permute-start.3 = (f32[18,128]{1,0:T(8,128)S(1)}, f32[18,128]{1,0:T(8,128)S(1)}, u32[]{:S(2)}, u32[]{:S(2)}) collective-permute-start(f32[18,128]{1,0:T(8,128)S(1)} %get-tuple-element.53), channel_id=1, source_target_pairs={{0,3},{1,0},{2,1},{3,2},{4,7},{5,4},{6,5},{7,6},{8,11},{9,8},{10,9... | collective-permute-start | bytes 27656 | tf_op jit(solution)/shard_map/ppermute | solution.py:467
  28.1 0.0 collective-permute-done.1.refs_1_
  28.1 0.8 %collective-permute-done.2.refs_2_ = f32[18,128]{1,0:T(8,128)S(1)} collective-permute-done((f32[18,128]{1,0:T(8,128)S(1)}, f32[18,128]{1,0:T(8,128)S(1)}, u32[]{:S(2)}, u32[]{:S(2)}) %collective-permute-start.2) | collective-permute-done | bytes 9248 | tf_op jit(solution)/shard_map/ppermute | solution.py:467
  28.9 0.6 %collective-permute-done.3.refs_3_ = f32[18,128]{1,0:T(8,128)S(1)} collective-permute-done((f32[18,128]{1,0:T(8,128)S(1)}, f32[18,128]{1,0:T(8,128)S(1)}, u32[]{:S(2)}, u32[]{:S(2)}) %collective-permute-start.3) | collective-permute-done | bytes 9248 | tf_op jit(solution)/shard_map/ppermute | solution.py:467
  29.5 3.7 %all-to-all-done.1 = f32[32,9,1,128]{3,2,1,0:T(1,128)S(1)} async-done(((f32[32,9,1,128]{3,2,1,0:T(1,128)}), f32[32,9,1,128]{3,2,1,0:T(1,128)S(1)}, u32[]{:S(2)}, u32[]{:S(2)}) %all-to-all-start.1) | async-done | bytes 147488 | tf_op jit(solution)/shard_map/all_to_all | solution.py:360
  33.2 0.3 image.1
  33.5 9.9 %all_to_all.15 = f32[32,7,1,128]{3,2,1,0:T(1,128)S(1)} all-to-all(f32[32,7,1,128]{3,2,1,0:T(1,128)S(1)} %bitcast.36), channel_id=1, replica_groups=mesh['nodes'=8,'cams'=4] {'nodes','cams'}, dimensions={0} | all-to-all | bytes 229376 | tf_op jit(solution)/shard_map/all_to_all | solution.py:360
  43.4 0.0 copy-done
  43.5 0.0 copy-done.1
  43.5 0.0 copy-done.2
  43.5 0.0 copy-done.3
  43.5 0.7 %update.1 = (f32[24,128]{1,0:T(8,128)}, f32[24,128]{1,0:T(8,128)}, f32[24,128]{1,0:T(8,128)}) custom-call(f32[224,128]{1,0:T(8,128)S(1)} %bitcast.35, f32[24,128]{1,0:T(8,128)S(1)} %bitcast.46, f32[24,128]{1,0:T(8,128)S(1)} %bitcast.45, f32[24,128]{1,0:T(8,128)S(1)} %bitcast.40, f32[24,128]{1,0:T(8,128)S(1)} %bitcast.43), custom_call_target="tpu_custom_call" | custom-call | tf_op jit(solution)/shard_map/update/pallas_call | solution.py:479
Async XLA Ops:
  2.1 16.7 %all-to-all-start = ((f32[32,13,1,128]{3,2,1,0:T(1,128)}), f32[32,13,1,128]{3,2,1,0:T(1,128)S(1)}, u32[]{:S(2)}, u32[]{:S(2)}) async-start(f32[32,13,1,128]{3,2,1,0:T(1,128)} %bitcast.8), calls=%async_computation | async-start | bytes 425984 | tf_op jit(solution)/shard_map/all_to_all | solution.py:360
  10.2 0.7 %copy-start.4 = (s32[1,8,3]{1,0,2:T(1,128)S(1)}, s32[1,8,3]{1,0,2:T(1,128)}, u32[]{:S(2)}) copy-start(s32[1,8,3]{1,0,2:T(1,128)} %param.13) | copy-start | bytes 292
  19.2 1.3 %collective-permute-start = (f32[192,128]{1,0:T(8,128)S(1)}, f32[192,128]{1,0:T(8,128)S(1)}, u32[]{:S(2)}, u32[]{:S(2)}) collective-permute-start(f32[192,128]{1,0:T(8,128)S(1)} %get-tuple-element.37.table), channel_id=1, source_target_pairs={{0,1},{1,0},{2,3},{3,2},{4,5},{5,4},{6,7},{7,6},{8,9},{9,8},{10,11... | collective-permute-start | bytes 294920 | tf_op jit(solution)/shard_map/ppermute | solution.py:444
  20.0 23.4 %copy-start = (f32[2,12,128]{2,0,1:T(2,128)S(1)}, f32[2,12,128]{2,0,1:T(2,128)}, u32[]{:S(2)}) copy-start(f32[2,12,128]{2,0,1:T(2,128)} %param.11) | copy-start | bytes 36868
  20.0 23.4 %copy-start.1 = (f32[2,12,128]{2,0,1:T(2,128)S(1)}, f32[2,12,128]{2,0,1:T(2,128)}, u32[]{:S(2)}) copy-start(f32[2,12,128]{2,0,1:T(2,128)} %param.12) | copy-start | bytes 36868
  20.1 23.4 %copy-start.2 = (f32[2,12,128]{2,0,1:T(2,128)S(1)}, f32[2,12,128]{2,0,1:T(2,128)}, u32[]{:S(2)}) copy-start(f32[2,12,128]{2,0,1:T(2,128)} %param.10) | copy-start | bytes 36868
  20.1 23.4 %copy-start.3 = (f32[2,12,128]{2,0,1:T(2,128)S(1)}, f32[2,12,128]{2,0,1:T(2,128)}, u32[]{:S(2)}) copy-start(f32[2,12,128]{2,0,1:T(2,128)} %param.9) | copy-start | bytes 36868
  22.2 11.0 %all-to-all-start.1 = ((f32[32,9,1,128]{3,2,1,0:T(1,128)}), f32[32,9,1,128]{3,2,1,0:T(1,128)S(1)}, u32[]{:S(2)}, u32[]{:S(2)}) async-start(f32[32,9,1,128]{3,2,1,0:T(1,128)} %bitcast.10), calls=%async_computation.1 | async-start | bytes 294912 | tf_op jit(solution)/shard_map/all_to_all | solution.py:360
  24.8 3.3 %collective-permute-start.1 = (f32[18,128]{1,0:T(8,128)S(1)}, f32[18,128]{1,0:T(8,128)S(1)}, u32[]{:S(2)}, u32[]{:S(2)}) collective-permute-start(f32[18,128]{1,0:T(8,128)S(1)} %get-tuple-element.51), channel_id=1, source_target_pairs={{0,1},{1,2},{2,3},{3,0},{4,5},{5,6},{6,7},{7,4},{8,9},{9,10},{10,1... | collective-permute-start | bytes 27656 | tf_op jit(solution)/shard_map/ppermute | solution.py:467
  25.1 3.8 %collective-permute-start.2 = (f32[18,128]{1,0:T(8,128)S(1)}, f32[18,128]{1,0:T(8,128)S(1)}, u32[]{:S(2)}, u32[]{:S(2)}) collective-permute-start(f32[18,128]{1,0:T(8,128)S(1)} %get-tuple-element.52), channel_id=1, source_target_pairs={{0,2},{1,3},{2,0},{3,1},{4,6},{5,7},{6,4},{7,5},{8,10},{9,11},{10,... | collective-permute-start | bytes 27656 | tf_op jit(solution)/shard_map/ppermute | solution.py:467
  26.8 2.7 %collective-permute-start.3 = (f32[18,128]{1,0:T(8,128)S(1)}, f32[18,128]{1,0:T(8,128)S(1)}, u32[]{:S(2)}, u32[]{:S(2)}) collective-permute-start(f32[18,128]{1,0:T(8,128)S(1)} %get-tuple-element.53), channel_id=1, source_target_pairs={{0,3},{1,0},{2,1},{3,2},{4,7},{5,4},{6,5},{7,6},{8,11},{9,8},{10,9... | collective-permute-start | bytes 27656 | tf_op jit(solution)/shard_map/ppermute | solution.py:467

commit v5 on v4

--- a/solution.py
+++ b/solution.py
@@ -226,7 +226,7 @@
 def own_kernel(table, masked, pulled_out):
     parity = lax.rem(lax.axis_index("cams"), 2)
     turned_table = turned_halves(table)
-    chunk = min(1024, masked.shape[1])
+    chunk = min(2048, masked.shape[1])
     for at in range(0, masked.shape[1], chunk):
         cols = slice(at, at + chunk)
         pulled_out[:, cols] = pull(turned_table, masked, parity, cols)
@@ -238,7 +238,7 @@
     parity = 1 - lax.rem(lax.axis_index("cams"), 2)
     turned_table = turned_halves(table)
     squares = jnp.zeros((1, LANES), f32)
-    chunk = min(1024, masked.shape[1])
+    chunk = min(2048, masked.shape[1])
     for at in range(0, spread.shape[1], chunk):
         cols = slice(at, at + chunk)
         weights = spread[:, cols]

time: 44.7 us -> 44.8 us (level)
  no operation moved by 1% of the time
where the time goes in v5:
time: 44.8 us; the launch traced here: 44.2 us
  starting transfers between devices  13.6 us (30%)
  waiting for transfers between devices  10.5 us (23%)
  blocking collectives  9.95 us (22%)
  Pallas kernels  6.32 us (14%)
  other arithmetic  2.41 us (5%)
  between operations  0.73 us (2%)
  local copies, waits for them, and re-layouts  0.7 us (2%)
    all_to_all x1, blocking collectives, exchange(): lax.all_to_all(blocks, axes, split_axis=0, concat_axis=0, tiled=True)  9.95 us
    all_to_all x2, starting transfers between devices, exchange(): lax.all_to_all(blocks, axes, split_axis=0, concat_axis=0, tiled=True)  9.88 us
    all_to_all x2, waiting for transfers between devices, exchange(): lax.all_to_all(blocks, axes, split_axis=0, concat_axis=0, tiled=True)  8.71 us
    ppermute x3, starting transfers between devices, on_device(): mine.append(lax.ppermute(pieces[distance], 'cams', turn))  3.3 us
    add x3, other arithmetic, joined_rows(): total = value if total is None else total + value  2.41 us
    pallas_call x1, Pallas kernels, on_device(): pl.pallas_call(functools.partial(data_kernel, sizes), out_shape=(array(de...  1.73 us
    ppermute x3, waiting for transfers between devices, on_device(): mine.append(lax.ppermute(pieces[distance], 'cams', turn))  1.4 us
    pallas_call x1, Pallas kernels, on_device(): pl.pallas_call(functools.partial(masks_kernel, params, node_refs.shape[0]...  1.15 us
  transfers between devices with their start and end apart: 6, of which 5 were waited for; matrix products, arithmetic and copies ran while one was open for 4% of the time, Pallas kernels for 6%

profile of v5, /device:TPU:0, one launch (start us, length us, event | category | flops | bytes accessed | tf_op | source)
XLA Modules:
  0.0 44.2 jit_solution(4373401637088770849)
XLA Ops:
  0.6 0.7 %convert_add_fusion.2 = f32[32,1,128]{2,1,0:T(1,128)S(1)} fusion(s32[3,1,8]{2,1,0:T(1,128)} %bitcast.47, f32[24,1,128]{2,1,0:T(1,128)} %bitcast.38), kind=kLoop, calls=%fused_computation.2 | loop fusion | flops 8192 | bytes 28768 | tf_op jit(solution)/shard_map/add | solution.py:351
  1.4 0.8 %pack.1 = f32[416,128]{1,0:T(8,128)} custom-call(f32[32,128]{1,0:T(8,128)S(1)} %bitcast.41), custom_call_target="tpu_custom_call" | custom-call | tf_op jit(solution)/shard_map/pack/pallas_call | solution.py:391
  2.1 7.3 %all-to-all-start = ((f32[32,13,1,128]{3,2,1,0:T(1,128)}), f32[32,13,1,128]{3,2,1,0:T(1,128)S(1)}, u32[]{:S(2)}, u32[]{:S(2)}) async-start(f32[32,13,1,128]{3,2,1,0:T(1,128)} %bitcast.8), calls=%async_computation | async-start | bytes 425984 | tf_op jit(solution)/shard_map/all_to_all | solution.py:360
  9.5 0.8 %convert_add_fusion.1 = f32[48,2,128]{2,1,0:T(2,128)S(1)} fusion(s32[6,2,128]{2,1,0:T(2,128)} %bitcast.49, f32[12,2,128]{2,1,0:T(2,128)} %bitcast.42, f32[12,2,128]{2,1,0:T(2,128)} %bitcast.44, f32[12,2,128]{2,1,0:T(2,128)} %bitcast.39), kind=kLoop, calls=%fused_computation.1 | loop fusion | flops 49152 | bytes 92160 | tf_op jit(solution)/shard_map/add | solution.py:351
  10.2 0.0 copy-start.4
  10.2 0.7 %copy-done.4 = s32[1,8,3]{1,0,2:T(1,128)S(1)} copy-done((s32[1,8,3]{1,0,2:T(1,128)S(1)}, s32[1,8,3]{1,0,2:T(1,128)}, u32[]{:S(2)}) %copy-start.4) | copy-done | bytes 120
  10.9 0.8 %near.1 = (f32[8,128]{1,0:T(8,128)S(1)}, bf16[32,288]{1,0:T(8,128)(2,1)S(1)}, f32[18,128]{1,0:T(8,128)S(1)}, f32[18,128]{1,0:T(8,128)S(1)}, f32[18,128]{1,0:T(8,128)S(1)}, /*index=5*/f32[18,128]{1,0:T(8,128)S(1)}) custom-call(s32[3,1,8]{2,1,0:T(1,128)S(1)} %bitcast.48, f32[96,128]{1,0:T(8,128)S(1)} %bitcast.37), custom_call_target="tpu_custom_call" | custom-call | tf_op jit(solution)/shard_map/near/pallas_call | solution.py:413
  11.8 0.9 %convert_add_fusion.pixel_rows = f32[24,2048]{1,0:T(8,128)S(1)} fusion(s32[4,2048]{1,0:T(4,128)} %param.15, bf16[4,2048]{1,0:T(4,128)(2,1)} %param.16, bf16[12,2048]{1,0:T(8,128)(2,1)} %param.14), kind=kLoop, calls=%fused_computation | loop fusion | flops 245760 | bytes 294912 | tf_op jit(solution)/shard_map/add | solution.py:351
  12.7 1.1 %masks.1 = (f32[128,2048]{1,0:T(8,128)S(1)}, bf16[384,2048]{1,0:T(8,128)(2,1)S(1)}) custom-call(f32[24,2048]{1,0:T(8,128)S(1)} %convert_add_fusion.pixel_rows), custom_call_target="tpu_custom_call" | custom-call | tf_op jit(solution)/shard_map/masks/pallas_call | solution.py:423
  13.8 5.0 %all-to-all-done = f32[32,13,1,128]{3,2,1,0:T(1,128)S(1)} async-done(((f32[32,13,1,128]{3,2,1,0:T(1,128)}), f32[32,13,1,128]{3,2,1,0:T(1,128)S(1)}, u32[]{:S(2)}, u32[]{:S(2)}) %all-to-all-start) | async-done | bytes 213024 | tf_op jit(solution)/shard_map/all_to_all | solution.py:360
  18.8 0.3 table.1
  19.2 0.4 collective-permute-start
  19.6 0.5 %own_half.1.pulled_own = f32[128,2048]{1,0:T(8,128)S(1)} custom-call(f32[192,128]{1,0:T(8,128)S(1)} %get-tuple-element.37.table, bf16[384,2048]{1,0:T(8,128)(2,1)S(1)} %get-tuple-element.38.masked), custom_call_target="tpu_custom_call" | custom-call | tf_op jit(solution)/shard_map/own_half/pallas_call | solution.py:445
  20.0 0.0 copy-start
  20.0 0.0 copy-start.1
  20.1 0.0 copy-start.2
  20.1 0.0 copy-start.3
  20.1 0.4 collective-permute-done.table
  20.5 1.7 %data_products.1 = (f32[288,128]{1,0:T(8,128)}, f32[8,128]{1,0:T(8,128)S(1)}) custom-call(f32[128,2048]{1,0:T(8,128)S(1)} %own_half.1.pulled_own, f32[192,128]{1,0:T(8,128)S(1)} %collective-permute-done.table, f32[128,2048]{1,0:T(8,128)S(1)} %get-tuple-element.39.spread, bf16[384,2048]{1,0:T(8,128)(2,1)S(1)} %get-tuple-element.38.masked), custom_call_target="tpu_custom_call" | custom-call | tf_op jit(solution)/shard_map/data_products/pallas_call | solution.py:453
  22.2 2.6 %all-to-all-start.1 = ((f32[32,9,1,128]{3,2,1,0:T(1,128)}), f32[32,9,1,128]{3,2,1,0:T(1,128)S(1)}, u32[]{:S(2)}, u32[]{:S(2)}) async-start(f32[32,9,1,128]{3,2,1,0:T(1,128)} %bitcast.10), calls=%async_computation.1 | async-start | bytes 294912 | tf_op jit(solution)/shard_map/all_to_all | solution.py:360
  24.8 0.3 collective-permute-start.1
  25.1 1.7 %collective-permute-start.2 = (f32[18,128]{1,0:T(8,128)S(1)}, f32[18,128]{1,0:T(8,128)S(1)}, u32[]{:S(2)}, u32[]{:S(2)}) collective-permute-start(f32[18,128]{1,0:T(8,128)S(1)} %get-tuple-element.52), channel_id=1, source_target_pairs={{0,2},{1,3},{2,0},{3,1},{4,6},{5,7},{6,4},{7,5},{8,10},{9,11},{10,... | collective-permute-start | bytes 27656 | tf_op jit(solution)/shard_map/ppermute | solution.py:467
  26.8 1.3 %collective-permute-start.3 = (f32[18,128]{1,0:T(8,128)S(1)}, f32[18,128]{1,0:T(8,128)S(1)}, u32[]{:S(2)}, u32[]{:S(2)}) collective-permute-start(f32[18,128]{1,0:T(8,128)S(1)} %get-tuple-element.53), channel_id=1, source_target_pairs={{0,3},{1,0},{2,1},{3,2},{4,7},{5,4},{6,5},{7,6},{8,11},{9,8},{10,9... | collective-permute-start | bytes 27656 | tf_op jit(solution)/shard_map/ppermute | solution.py:467
  28.1 0.0 collective-permute-done.1.refs_1_
  28.1 0.8 %collective-permute-done.2.refs_2_ = f32[18,128]{1,0:T(8,128)S(1)} collective-permute-done((f32[18,128]{1,0:T(8,128)S(1)}, f32[18,128]{1,0:T(8,128)S(1)}, u32[]{:S(2)}, u32[]{:S(2)}) %collective-permute-start.2) | collective-permute-done | bytes 9248 | tf_op jit(solution)/shard_map/ppermute | solution.py:467
  28.9 0.6 %collective-permute-done.3.refs_3_ = f32[18,128]{1,0:T(8,128)S(1)} collective-permute-done((f32[18,128]{1,0:T(8,128)S(1)}, f32[18,128]{1,0:T(8,128)S(1)}, u32[]{:S(2)}, u32[]{:S(2)}) %collective-permute-start.3) | collective-permute-done | bytes 9248 | tf_op jit(solution)/shard_map/ppermute | solution.py:467
  29.5 3.7 %all-to-all-done.1 = f32[32,9,1,128]{3,2,1,0:T(1,128)S(1)} async-done(((f32[32,9,1,128]{3,2,1,0:T(1,128)}), f32[32,9,1,128]{3,2,1,0:T(1,128)S(1)}, u32[]{:S(2)}, u32[]{:S(2)}) %all-to-all-start.1) | async-done | bytes 147488 | tf_op jit(solution)/shard_map/all_to_all | solution.py:360
  33.2 0.3 image.1
  33.5 9.9 %all_to_all.15 = f32[32,7,1,128]{3,2,1,0:T(1,128)S(1)} all-to-all(f32[32,7,1,128]{3,2,1,0:T(1,128)S(1)} %bitcast.36), channel_id=1, replica_groups=mesh['nodes'=8,'cams'=4] {'nodes','cams'}, dimensions={0} | all-to-all | bytes 229376 | tf_op jit(solution)/shard_map/all_to_all | solution.py:360
  43.5 0.0 copy-done
  43.5 0.0 copy-done.1
  43.5 0.0 copy-done.2
  43.5 0.0 copy-done.3
  43.5 0.7 %update.1 = (f32[24,128]{1,0:T(8,128)}, f32[24,128]{1,0:T(8,128)}, f32[24,128]{1,0:T(8,128)}) custom-call(f32[224,128]{1,0:T(8,128)S(1)} %bitcast.35, f32[24,128]{1,0:T(8,128)S(1)} %bitcast.46, f32[24,128]{1,0:T(8,128)S(1)} %bitcast.45, f32[24,128]{1,0:T(8,128)S(1)} %bitcast.40, f32[24,128]{1,0:T(8,128)S(1)} %bitcast.43), custom_call_target="tpu_custom_call" | custom-call | tf_op jit(solution)/shard_map/update/pallas_call | solution.py:479
Async XLA Ops:
  2.1 16.7 %all-to-all-start = ((f32[32,13,1,128]{3,2,1,0:T(1,128)}), f32[32,13,1,128]{3,2,1,0:T(1,128)S(1)}, u32[]{:S(2)}, u32[]{:S(2)}) async-start(f32[32,13,1,128]{3,2,1,0:T(1,128)} %bitcast.8), calls=%async_computation | async-start | bytes 425984 | tf_op jit(solution)/shard_map/all_to_all | solution.py:360
  10.2 0.7 %copy-start.4 = (s32[1,8,3]{1,0,2:T(1,128)S(1)}, s32[1,8,3]{1,0,2:T(1,128)}, u32[]{:S(2)}) copy-start(s32[1,8,3]{1,0,2:T(1,128)} %param.13) | copy-start | bytes 292
  19.2 1.3 %collective-permute-start = (f32[192,128]{1,0:T(8,128)S(1)}, f32[192,128]{1,0:T(8,128)S(1)}, u32[]{:S(2)}, u32[]{:S(2)}) collective-permute-start(f32[192,128]{1,0:T(8,128)S(1)} %get-tuple-element.37.table), channel_id=1, source_target_pairs={{0,1},{1,0},{2,3},{3,2},{4,5},{5,4},{6,7},{7,6},{8,9},{9,8},{10,11... | collective-permute-start | bytes 294920 | tf_op jit(solution)/shard_map/ppermute | solution.py:444
  20.0 23.4 %copy-start = (f32[2,12,128]{2,0,1:T(2,128)S(1)}, f32[2,12,128]{2,0,1:T(2,128)}, u32[]{:S(2)}) copy-start(f32[2,12,128]{2,0,1:T(2,128)} %param.11) | copy-start | bytes 36868
  20.0 23.4 %copy-start.1 = (f32[2,12,128]{2,0,1:T(2,128)S(1)}, f32[2,12,128]{2,0,1:T(2,128)}, u32[]{:S(2)}) copy-start(f32[2,12,128]{2,0,1:T(2,128)} %param.12) | copy-start | bytes 36868
  20.1 23.4 %copy-start.2 = (f32[2,12,128]{2,0,1:T(2,128)S(1)}, f32[2,12,128]{2,0,1:T(2,128)}, u32[]{:S(2)}) copy-start(f32[2,12,128]{2,0,1:T(2,128)} %param.10) | copy-start | bytes 36868
  20.1 23.4 %copy-start.3 = (f32[2,12,128]{2,0,1:T(2,128)S(1)}, f32[2,12,128]{2,0,1:T(2,128)}, u32[]{:S(2)}) copy-start(f32[2,12,128]{2,0,1:T(2,128)} %param.9) | copy-start | bytes 36868
  22.2 11.0 %all-to-all-start.1 = ((f32[32,9,1,128]{3,2,1,0:T(1,128)}), f32[32,9,1,128]{3,2,1,0:T(1,128)S(1)}, u32[]{:S(2)}, u32[]{:S(2)}) async-start(f32[32,9,1,128]{3,2,1,0:T(1,128)} %bitcast.10), calls=%async_computation.1 | async-start | bytes 294912 | tf_op jit(solution)/shard_map/all_to_all | solution.py:360
  24.8 3.3 %collective-permute-start.1 = (f32[18,128]{1,0:T(8,128)S(1)}, f32[18,128]{1,0:T(8,128)S(1)}, u32[]{:S(2)}, u32[]{:S(2)}) collective-permute-start(f32[18,128]{1,0:T(8,128)S(1)} %get-tuple-element.51), channel_id=1, source_target_pairs={{0,1},{1,2},{2,3},{3,0},{4,5},{5,6},{6,7},{7,4},{8,9},{9,10},{10,1... | collective-permute-start | bytes 27656 | tf_op jit(solution)/shard_map/ppermute | solution.py:467
  25.1 3.8 %collective-permute-start.2 = (f32[18,128]{1,0:T(8,128)S(1)}, f32[18,128]{1,0:T(8,128)S(1)}, u32[]{:S(2)}, u32[]{:S(2)}) collective-permute-start(f32[18,128]{1,0:T(8,128)S(1)} %get-tuple-element.52), channel_id=1, source_target_pairs={{0,2},{1,3},{2,0},{3,1},{4,6},{5,7},{6,4},{7,5},{8,10},{9,11},{10,... | collective-permute-start | bytes 27656 | tf_op jit(solution)/shard_map/ppermute | solution.py:467
  26.8 2.7 %collective-permute-start.3 = (f32[18,128]{1,0:T(8,128)S(1)}, f32[18,128]{1,0:T(8,128)S(1)}, u32[]{:S(2)}, u32[]{:S(2)}) collective-permute-start(f32[18,128]{1,0:T(8,128)S(1)} %get-tuple-element.53), channel_id=1, source_target_pairs={{0,3},{1,0},{2,1},{3,2},{4,7},{5,4},{6,5},{7,6},{8,11},{9,8},{10,9... | collective-permute-start | bytes 27656 | tf_op jit(solution)/shard_map/ppermute | solution.py:467
